TPU v7x, 32 devices: a whole 2x2x4 slice. The times are simulated.
32 devices in a mesh: dp: 4 (over z), section: 4 (over x, core), et: 2 (over y).
Axes of the slice: x: 2, y: 2, z: 4, core: 2. Of those that a mesh axis runs over, the one named last changes fastest.
Arguments:
- handoff: bfloat16 [4, 1024, 3072], P('section', ('dp', 'et')), may hold values from -6 to 6
- fwd_slot: int32 [4, 1024], P('section', ('dp', 'et')), may hold values from -1 to 31, as said below
- fwd_weight: float32 [4, 1024], P('section', ('dp', 'et')), may hold values from 0.2 to 1
- stashed: bfloat16 [4, 1024, 3072], P('section', ('dp', 'et')), may hold values from -6 to 6
- back_slot: int32 [4, 1024], P('section', ('dp', 'et')), may hold values from -1 to 31, as said below
- back_weight: float32 [4, 1024], P('section', ('dp', 'et')), may hold values from 0.2 to 1
- grad_handoff: bfloat16 [4, 1024, 3072], P('section', ('dp', 'et')), may hold values from -6 to 6
- w_gate: bfloat16 [4, 3072, 5376], P('section', None, 'et'), may hold values from -0.109375 to 0.109375
- w_up: bfloat16 [4, 3072, 5376], P('section', None, 'et'), may hold values from -0.109375 to 0.109375
- w_down: bfloat16 [4, 5376, 3072], P('section', 'et'), may hold values from -0.078125 to 0.078125
Outputs:
- forward_out: bfloat16 [4, 1024, 3072], P('section', ('dp', 'et'))
- input_grad: bfloat16 [4, 1024, 3072], P('section', ('dp', 'et'))
- gate_grad: bfloat16 [4, 3072, 5376], P('section', 'dp', 'et')
- up_grad: bfloat16 [4, 3072, 5376], P('section', 'dp', 'et')
- down_grad: bfloat16 [4, 5376, 3072], P('section', 'et', 'dp')
Inputs may be any that keep to these rules, and one draw needn't show every extreme that they name: `fwd_slot`: within each group of 128 rows of one device, the tokens routed to the expert carry the slots 0, 1, 2, ... in the order of the rows and the others carry -1; at least a quarter of 32 are routed; some device has exactly 32 routed tokens. `back_slot`: as for fwd_slot.
All inputs are finite; a program needn't handle non-finite values.
Results may differ from a plain program's by a relative error of at most 0.02.
Values may be sent and summed in bfloat16 or wider, within the bound.
A program may use at most 192 MiB of HBM per device.

v0:
```python
import jax
import jax.numpy as jnp
from jax import lax
from jax.sharding import PartitionSpec as P

CAP = 32


def passed_along(block, axis, distance):
    devices = range(lax.axis_size(axis))
    route = [((i - distance) % len(devices), i) for i in devices]
    return lax.ppermute(block, axis, route)


def pack_rows(row_block, slot_ids):
    places = lax.broadcasted_iota(jnp.int32, (CAP, slot_ids.shape[0]), 0)
    picker = (places == slot_ids[None, :]).astype(jnp.bfloat16)
    return jnp.dot(picker, row_block, preferred_element_type=jnp.float32).astype(jnp.bfloat16)


def unpack_rows(packed, slot_ids):
    places = lax.broadcasted_iota(jnp.int32, (slot_ids.shape[0], CAP), 1)
    picker = (places == slot_ids[:, None]).astype(jnp.float32)
    return jnp.dot(
        picker, packed, precision=lax.Precision.HIGHEST, preferred_element_type=jnp.float32
    )


def activations(row_block, gate_w, up_w):
    pre_gate = jnp.dot(row_block, gate_w, preferred_element_type=jnp.float32)
    pre_up = jnp.dot(row_block, up_w, preferred_element_type=jnp.float32)
    sigmoid_gate = jax.nn.sigmoid(pre_gate)
    active = pre_gate * sigmoid_gate
    hidden = (active * pre_up).astype(jnp.bfloat16)
    return (pre_gate, pre_up, sigmoid_gate, active, hidden)


def forward_pass(fwd_rows, slot_ids, weights_row, gate_w, up_w, down_w):
    hidden = activations(fwd_rows, gate_w, up_w)[4]
    own_sum = lax.psum_scatter(
        jnp.dot(hidden, down_w, preferred_element_type=jnp.float32).astype(jnp.bfloat16),
        "et",
        scatter_dimension=0,
        tiled=True,
    ).astype(jnp.float32)
    return (weights_row[:, None] * unpack_rows(own_sum, slot_ids)).astype(jnp.bfloat16)


def backward_pass(back_rows, grad_rows_all, slot_ids, gate_w, up_w, down_w):
    pre_gate, pre_up, sigmoid_gate, active, hidden = activations(back_rows, gate_w, up_w)
    contract_last = (((1,), (1,)), ((), ()))
    contract_first = (((0,), (0,)), ((), ()))
    grad_hidden = lax.dot_general(
        grad_rows_all, down_w, contract_last, preferred_element_type=jnp.float32
    )
    grad_upact = (grad_hidden * active).astype(jnp.bfloat16)
    grad_gateact = (
        grad_hidden * pre_up * sigmoid_gate * (1.0 + pre_gate * (1.0 - sigmoid_gate))
    ).astype(jnp.bfloat16)
    gate_term = lax.dot_general(
        back_rows, grad_gateact, contract_first, preferred_element_type=jnp.float32
    )
    up_term = lax.dot_general(
        back_rows, grad_upact, contract_first, preferred_element_type=jnp.float32
    )
    down_term = lax.dot_general(
        hidden, grad_rows_all, contract_first, preferred_element_type=jnp.float32
    )
    from_gate = lax.dot_general(
        grad_gateact, gate_w, contract_last, preferred_element_type=jnp.float32
    )
    from_up = lax.dot_general(grad_upact, up_w, contract_last, preferred_element_type=jnp.float32)
    own_grad = lax.psum_scatter(
        (from_gate + from_up).astype(jnp.bfloat16), "et", scatter_dimension=0, tiled=True
    ).astype(jnp.float32)
    grad_rows = unpack_rows(own_grad, slot_ids).astype(jnp.bfloat16)
    weight_sums = (
        lax.psum_scatter(
            gate_term.astype(jnp.bfloat16), "dp", scatter_dimension=0, tiled=True
        ).astype(jnp.float32),
        lax.psum_scatter(
            up_term.astype(jnp.bfloat16), "dp", scatter_dimension=0, tiled=True
        ).astype(jnp.float32),
        lax.psum_scatter(
            down_term.astype(jnp.bfloat16), "dp", scatter_dimension=1, tiled=True
        ).astype(jnp.float32),
    )
    return (grad_rows, weight_sums)


def per_device(
    handoff,
    fwd_slot,
    fwd_weight,
    stashed,
    back_slot,
    back_weight,
    grad_handoff,
    w_gate,
    w_up,
    w_down,
):
    gate_w, up_w, down_w = (w_gate[0], w_up[0], w_down[0])
    arrived = passed_along(handoff, "section", 1)[0]
    returned = passed_along(grad_handoff, "section", -1)[0]
    fwd_ids = fwd_slot[0]
    back_ids = back_slot[0]
    scaled = (back_weight[0][:, None] * returned.astype(jnp.float32)).astype(jnp.bfloat16)
    fwd_packed = pack_rows(arrived, fwd_ids)
    stash_packed = pack_rows(stashed[0], back_ids)
    grad_packed = pack_rows(scaled, back_ids)
    fwd_rows = lax.all_gather(fwd_packed, "et", axis=0, tiled=True)
    back_rows, grad_rows_all = (
        lax.all_gather(stash_packed, "et", axis=0, tiled=True),
        lax.all_gather(grad_packed, "et", axis=0, tiled=True),
    )
    forward_out = forward_pass(fwd_rows, fwd_ids, fwd_weight[0], gate_w, up_w, down_w)
    grad_rows, weight_sums = backward_pass(back_rows, grad_rows_all, back_ids, gate_w, up_w, down_w)
    gate_sum, up_sum, down_sum = weight_sums
    return (
        forward_out[None],
        grad_rows[None],
        gate_sum.astype(jnp.bfloat16)[None],
        up_sum.astype(jnp.bfloat16)[None],
        down_sum.astype(jnp.bfloat16)[None],
    )


def solution(mesh):
    placed = (
        P("section", ("dp", "et"), None),
        P("section", ("dp", "et")),
        P("section", ("dp", "et")),
        P("section", ("dp", "et"), None),
        P("section", ("dp", "et")),
        P("section", ("dp", "et")),
        P("section", ("dp", "et"), None),
        P("section", None, "et"),
        P("section", None, "et"),
        P("section", "et", None),
    )
    return jax.shard_map(
        per_device,
        mesh=mesh,
        in_specs=placed,
        out_specs=(
            P("section", ("dp", "et"), None),
            P("section", ("dp", "et"), None),
            P("section", "dp", "et"),
            P("section", "dp", "et"),
            P("section", "et", "dp"),
        ),
        check_vma=False,
    )
```

profile of v0, /device:TPU:0, one launch (start us, length us, event | category | flops | bytes accessed | tf_op | source)
XLA Modules:
  0.0 975.3 jit_solution(11686555124056623476)
XLA Ops:
  7.2 2.4 collective-permute-start.1
  9.7 0.9 convolution_convert_fusion.4
  10.6 8.2 all_gather.11
  18.8 8.6 fusion.6
  27.4 0.5 collective-permute-done.1
  27.9 0.3 convolution_convert_fusion.5
  28.2 8.0 all_gather.10
  36.2 10.8 %fusion = f32[64,2688]{1,0:T(8,128)S(1)} fusion(bf16[64,3072]{1,0:T(8,128)(2,1)S(1)} %all_gather.10, bf16[1,2688,3072]{2,1,0:T(8,128)(2,1)} %param.19), kind=kOutput, calls=%fused_computation.3 | convolution fusion | flops 1056964608 | bytes 17596416 | tf_op jit(solution)/shard_map/dot_general | solution.py:53
  46.9 8.7 multiply_convert_fusion.2
  55.7 10.8 %fusion.4 = f32[64,3072]{1,0:T(8,128)S(1)} fusion(bf16[64,2688]{1,0:T(8,128)(2,1)S(1)} %get-tuple-element.6, bf16[1,3072,2688]{2,1,0:T(8,128)(2,1)} %param.18), kind=kOutput, calls=%fused_computation.7 | convolution fusion | flops 1056964608 | bytes 17645568 | tf_op jit(solution)/shard_map/dot_general | solution.py:72
  66.5 11.6 %fusion.28 = bf16[64,3072]{1,0:T(8,128)(2,1)} fusion(f32[64,3072]{1,0:T(8,128)S(1)} %fusion.4, bf16[64,2688]{1,0:T(8,128)(2,1)S(1)} %get-tuple-element.5, bf16[1,3072,2688]{2,1,0:T(8,128)(2,1)} %param.17), kind=kOutput, calls=%fused_computation.27 | convolution fusion | flops 1057357824 | bytes 18038784 | tf_op jit(solution)/shard_map/dot_general | solution.py:69
  78.1 1.4 convolution_convert_fusion.6
  79.5 8.0 all_gather.9
  87.5 9.5 fusion.14
  97.0 17.2 %fusion.25 = bf16[64,3072]{1,0:T(8,128)(2,1)} fusion(bf16[1,2688,3072]{2,1,0:T(8,128)(2,1)} %param.19, bf16[64,3072]{1,0:T(8,128)(2,1)S(1)} %all_gather.9, bf16[1,3072,2688]{2,1,0:T(8,128)(2,1)} %param.18, f32[64,2688]{1,0:T(8,128)} %fusion.14), kind=kOutput, calls=%fused_computation.26 | convolution fusion | flops 2115158016 | bytes 34504704 | tf_op jit(solution)/shard_map/dot_general | solution.py:41
  114.3 8.3 convolution_convert_fusion
  122.7 8.1 convolution_convert_fusion.2
  130.8 0.3 reduce-scatter.12.cloned.1.call-start
  131.1 8.3 convolution_convert_fusion.1
  139.5 2.3 fusion.18
  141.8 2.2 fusion.17
  144.0 265.4 %reduce-scatter.14.cloned.1.call-done = bf16[2688,768]{1,0:T(8,128)(2,1)} async-done(((bf16[2688,3072]{1,0:T(8,128)(2,1)}), bf16[2688,768]{1,0:T(8,128)(2,1)}) %reduce-scatter.14.cloned.1.call-update) | async-done | bytes 4128784 | tf_op jit(solution)/shard_map/reduce_scatter | solution.py:84
  409.3 279.8 %reduce-scatter.10.cloned.1.call-done = bf16[768,2688]{1,0:T(8,128)(2,1)} async-done(((bf16[3072,2688]{1,0:T(8,128)(2,1)}), bf16[768,2688]{1,0:T(8,128)(2,1)}) %reduce-scatter.10.cloned.1.call-update) | async-done | bytes 4128784 | tf_op jit(solution)/shard_map/reduce_scatter | solution.py:78
  689.1 279.6 %reduce-scatter.12.cloned.1.call-done = bf16[768,2688]{1,0:T(8,128)(2,1)} async-done(((bf16[3072,2688]{1,0:T(8,128)(2,1)}), bf16[768,2688]{1,0:T(8,128)(2,1)}) %reduce-scatter.12.cloned.1.call-update) | async-done | bytes 4128784 | tf_op jit(solution)/shard_map/reduce_scatter | solution.py:81
  (25 shorter events, 0.3 us)
Async XLA Ops:
  7.2 2.5 copy-start
  7.2 20.7 %copy-start.2 = (s32[1,128]{1,0:T(1,128)S(1)}, s32[1,128]{1,0:T(1,128)}, u32[]{:S(2)}) copy-start(s32[1,128]{1,0:T(1,128)} %param.14) | copy-start | bytes 1540
  7.2 20.7 %copy-start.4 = (f32[1,128]{1,0:T(1,128)S(1)}, f32[1,128]{1,0:T(1,128)}, u32[]{:S(2)}) copy-start(f32[1,128]{1,0:T(1,128)} %param.15) | copy-start | bytes 1540
  7.2 132.3 %reduce-scatter.8.cloned.1.call-start = ((), (), s32[]{:S(2)}) async-start(), calls=%async_computation.6 | async-start | bytes 589824 | tf_op jit(solution)/shard_map/reduce_scatter | solution.py:73
  7.2 20.6 %collective-permute-start.1 = (bf16[1,128,3072]{2,1,0:T(8,128)(2,1)}, bf16[1,128,3072]{2,1,0:T(8,128)(2,1)S(1)}, u32[]{:S(2)}, u32[]{:S(2)}) collective-permute-start(bf16[1,128,3072]{2,1,0:T(8,128)(2,1)} %param.16), channel_id=1, source_target_pairs={{2,0},{4,2},{6,4},{0,6},{3,1},{5,3},{7,5},{1,7},{10,8},{12,10},{14... | collective-permute-start | bytes 2359304 | tf_op jit(solution)/shard_map/ppermute | solution.py:12
  9.7 68.5 %collective-permute-start = (bf16[1,128,3072]{2,1,0:T(8,128)(2,1)}, bf16[1,128,3072]{2,1,0:T(8,128)(2,1)}, u32[]{:S(2)}, u32[]{:S(2)}) collective-permute-start(bf16[1,128,3072]{2,1,0:T(8,128)(2,1)} %param.10), channel_id=1, source_target_pairs={{6,0},{0,2},{2,4},{4,6},{7,1},{1,3},{3,5},{5,7},{14,8},{8,10},{10,... | collective-permute-start | bytes 2359304 | tf_op jit(solution)/shard_map/ppermute | solution.py:12
  55.7 22.4 %copy-start.3 = (s32[1,128]{1,0:T(1,128)S(1)}, s32[1,128]{1,0:T(1,128)}, u32[]{:S(2)}) copy-start(s32[1,128]{1,0:T(1,128)} %param.11) | copy-start | bytes 1540
  78.1 63.7 %reduce-scatter.6.cloned.1.call-start = ((), (), s32[]{:S(2)}) async-start(), calls=%async_computation.5 | async-start | bytes 589824 | tf_op jit(solution)/shard_map/reduce_scatter | solution.py:40
  114.3 295.0 %reduce-scatter.14.cloned.1.call-start = ((), (), s32[]{:S(2)}) async-start(), calls=%async_computation.9 | async-start | bytes 20643840 | tf_op jit(solution)/shard_map/reduce_scatter | solution.py:84
  122.6 566.5 %reduce-scatter.10.cloned.1.call-start = ((), (), s32[]{:S(2)}) async-start(), calls=%async_computation.7 | async-start | bytes 20643840 | tf_op jit(solution)/shard_map/reduce_scatter | solution.py:78
  130.8 11.0 %copy-start.5 = (f32[1,128]{1,0:T(1,128)S(1)}, f32[1,128]{1,0:T(1,128)}, u32[]{:S(2)}) copy-start(f32[1,128]{1,0:T(1,128)} %param.12) | copy-start | bytes 1540
  130.8 838.0 %copy-start.1 = (bf16[1,128,3072]{2,1,0:T(8,128)(2,1)S(1)}, bf16[1,128,3072]{2,1,0:T(8,128)(2,1)}, u32[]{:S(2)}) copy-start(bf16[1,128,3072]{2,1,0:T(8,128)(2,1)} %param.13) | copy-start | bytes 2359300
  130.8 838.0 %reduce-scatter.12.cloned.1.call-start = ((), (), s32[]{:S(2)}) async-start(), calls=%async_computation.8 | async-start | bytes 20643840 | tf_op jit(solution)/shard_map/reduce_scatter | solution.py:81
Sparse Core Ops, SparseCore 0:
  78.2 13.9 reduce-scatter.7
  114.4 15.7 reduce-scatter.5
  133.2 276.1 reduce-scatter.13
  412.3 276.8 reduce-scatter.9
  692.0 276.7 reduce-scatter.11
where the time goes:
time: 976 us; the launch traced here: 975 us
  waiting for transfers between devices  825 us (85%)
  matrix products  109 us (11%)
  blocking collectives  24.2 us (2%)
  between operations  13.9 us (1%)
    reduce_scatter x1, waiting for transfers between devices, backward_pass(): lax.psum_scatter(gate_term.astype(jnp.bfloat16), 'dp', scatter_dimension=...  280 us
    reduce_scatter x1, waiting for transfers between devices, backward_pass(): lax.psum_scatter(up_term.astype(jnp.bfloat16), 'dp', scatter_dimension=0,...  280 us
    reduce_scatter x1, waiting for transfers between devices, backward_pass(): lax.psum_scatter(down_term.astype(jnp.bfloat16), 'dp', scatter_dimension=...  265 us
  transfers between devices with their start and end apart: 7, of which 4 were waited for; matrix products, arithmetic and copies ran while one was open for 11% of the time, Pallas kernels for 0%

commit v1 on v0

v1 whole, which is shorter than its diff:
```python
import functools

import jax
import jax.numpy as jnp
from jax import lax
from jax.experimental import pallas as pl
from jax.experimental.pallas import tpu as pltpu
from jax.sharding import PartitionSpec as P

CAP = 32
NN = (((1,), (0,)), ((), ()))
NT = (((1,), (1,)), ((), ()))
TN = (((0,), (0,)), ((), ()))


def mul(a, b, dims=NN):
    return lax.dot_general(a, b, dims, preferred_element_type=jnp.float32)


def passed_along(block, axis, distance):
    n = lax.axis_size(axis)
    return lax.ppermute(block, axis, [((i - distance) % n, i) for i in range(n)])


def pack_rows(row_block, slot_ids):
    places = lax.broadcasted_iota(jnp.int32, (CAP, slot_ids.shape[0]), 0)
    picker = (places == slot_ids[None, :]).astype(jnp.bfloat16)
    return mul(picker, row_block).astype(jnp.bfloat16)


def pack_values(values, slot_ids):
    places = lax.broadcasted_iota(jnp.int32, (CAP, slot_ids.shape[0]), 0)
    return jnp.sum(jnp.where(places == slot_ids[None, :], values[None, :], 0.0), axis=1)


def unpack_rows(packed, slot_ids):
    places = lax.broadcasted_iota(jnp.int32, (slot_ids.shape[0], CAP), 1)
    picker = (places == slot_ids[:, None]).astype(jnp.float32)
    return jnp.dot(
        picker, packed, precision=lax.Precision.HIGHEST, preferred_element_type=jnp.float32
    )


def gather_et(rows):
    if lax.axis_size("et") == 2:
        return jnp.concatenate([rows, passed_along(rows, "et", 1)], axis=0)
    return lax.all_gather(rows, "et", axis=0, tiled=True)


def scatter_et(partial):
    if lax.axis_size("et") == 2:
        other = passed_along(partial[CAP:], "et", 1)
        return partial[:CAP].astype(jnp.float32) + other.astype(jnp.float32)
    return lax.psum_scatter(partial, "et", scatter_dimension=0, tiled=True).astype(jnp.float32)


def gates(pre_gate, pre_up, grad_hidden):
    sig = jax.nn.sigmoid(pre_gate)
    active = pre_gate * sig
    hidden = (active * pre_up).astype(jnp.bfloat16)
    grad_up = (grad_hidden * active).astype(jnp.bfloat16)
    grad_gate = (grad_hidden * pre_up * sig * (1.0 + pre_gate * (1.0 - sig))).astype(jnp.bfloat16)
    return hidden, grad_gate, grad_up


def back_kernel(
    own_rows,
    back_ref,
    grad_ref,
    back_cols_t,
    grad_cols,
    gate_ref,
    up_ref,
    down_ref,
    gate_out,
    up_out,
    down_out,
    rows_out,
    gate_act,
    up_act,
    total,
):
    step = pl.program_id(0)
    pre_gate = mul(back_ref[...], gate_ref[...])
    pre_up = mul(back_ref[...], up_ref[...])
    grad_hidden = mul(grad_ref[...], down_ref[...], NT)
    hidden, grad_gate, grad_up = gates(pre_gate, pre_up, grad_hidden)
    gate_act[...] = grad_gate
    up_act[...] = grad_up
    gate_out[...] = mul(back_cols_t[...], grad_gate).astype(jnp.bfloat16)
    up_out[...] = mul(back_cols_t[...], grad_up).astype(jnp.bfloat16)
    down_out[...] = mul(hidden, grad_cols[...], TN).astype(jnp.bfloat16)
    own = pl.ds(pl.multiple_of(lax.axis_index("dp") * own_rows, own_rows), own_rows)
    term = mul(gate_act[own, :], gate_ref[...], NT) + mul(up_act[own, :], up_ref[...], NT)

    @pl.when(step == 0)
    def _():
        total[...] = term

    @pl.when(step > 0)
    def _():
        total[...] += term

    @pl.when(step == pl.num_programs(0) - 1)
    def _():
        rows_out[...] = total[...].astype(jnp.bfloat16)


def backward(back_all, grad_all, back_cols, grad_cols, gate_w, up_w, down_w, tile):
    rows, depth = back_all.shape
    share = back_cols.shape[1]
    units = gate_w.shape[1]
    own_rows = rows // lax.axis_size("dp")
    whole = lambda i: (0, 0)
    once = functools.partial(pl.BlockSpec, index_map=whole, pipeline_mode=pl.Buffered(1))
    across = lambda i: (0, i)
    down = lambda i: (i, 0)
    flops = 2 * units * (3 * rows * depth + 2 * own_rows * depth + 3 * rows * share)
    return pl.pallas_call(
        functools.partial(back_kernel, own_rows),
        grid=(units // tile,),
        in_specs=[
            once((rows, depth)),
            once((rows, depth)),
            once((share, rows)),
            once((rows, share)),
            pl.BlockSpec((depth, tile), across),
            pl.BlockSpec((depth, tile), across),
            pl.BlockSpec((tile, depth), down),
        ],
        out_specs=[
            pl.BlockSpec((share, tile), across),
            pl.BlockSpec((share, tile), across),
            pl.BlockSpec((tile, share), down),
            pl.BlockSpec((own_rows, depth), whole),
        ],
        out_shape=[
            jax.ShapeDtypeStruct((share, units), jnp.bfloat16),
            jax.ShapeDtypeStruct((share, units), jnp.bfloat16),
            jax.ShapeDtypeStruct((units, share), jnp.bfloat16),
            jax.ShapeDtypeStruct((own_rows, depth), jnp.bfloat16),
        ],
        scratch_shapes=[
            pltpu.VMEM((rows, tile), jnp.bfloat16),
            pltpu.VMEM((rows, tile), jnp.bfloat16),
            pltpu.VMEM((own_rows, depth), jnp.float32),
        ],
        compiler_params=pltpu.CompilerParams(vmem_limit_bytes=48 * 2**20),
        cost_estimate=pl.CostEstimate(
            flops=flops,
            bytes_accessed=6 * units * (depth + share) + 8 * rows * depth,
            transcendentals=rows * units,
        ),
    )(back_all, grad_all, back_cols.T, grad_cols, gate_w, up_w, down_w)


def backward_plain(back_all, grad_all, back_cols, grad_cols, gate_w, up_w, down_w):
    pre_gate, pre_up = mul(back_all, gate_w), mul(back_all, up_w)
    hidden, grad_gate, grad_up = gates(pre_gate, pre_up, mul(grad_all, down_w, NT))
    own_rows = back_all.shape[0] // lax.axis_size("dp")
    start = lax.axis_index("dp") * own_rows
    own_gate = lax.dynamic_slice_in_dim(grad_gate, start, own_rows, 0)
    own_up = lax.dynamic_slice_in_dim(grad_up, start, own_rows, 0)
    return (
        mul(back_cols, grad_gate, TN).astype(jnp.bfloat16),
        mul(back_cols, grad_up, TN).astype(jnp.bfloat16),
        mul(hidden, grad_cols, TN).astype(jnp.bfloat16),
        (mul(own_gate, gate_w, NT) + mul(own_up, up_w, NT)).astype(jnp.bfloat16),
    )


def per_device(
    handoff,
    fwd_slot,
    fwd_weight,
    stashed,
    back_slot,
    back_weight,
    grad_handoff,
    w_gate,
    w_up,
    w_down,
):
    gate_w, up_w, down_w = (w_gate[0], w_up[0], w_down[0])
    fwd_ids, back_ids = fwd_slot[0], back_slot[0]
    back_ids_there = passed_along(back_slot, "section", 1)[0]
    fwd_ids_there = passed_along(fwd_slot, "section", -1)[0]
    stash_packed = pack_rows(stashed[0], back_ids)
    back_all = lax.all_gather(stash_packed, ("dp", "et"), axis=0, tiled=True)
    returned = passed_along(pack_rows(grad_handoff[0], back_ids_there), "section", -1)
    weights = pack_values(back_weight[0], back_ids)
    grad_packed = (weights[:, None] * returned.astype(jnp.float32)).astype(jnp.bfloat16)
    grad_all = lax.all_gather(grad_packed, ("dp", "et"), axis=0, tiled=True)

    arrived = passed_along(pack_rows(handoff[0], fwd_ids_there), "section", 1)
    fwd_rows = gather_et(arrived)
    pre_gate = mul(fwd_rows, gate_w)
    pre_up = mul(fwd_rows, up_w)
    hidden = (pre_gate * jax.nn.sigmoid(pre_gate) * pre_up).astype(jnp.bfloat16)
    own_sum = scatter_et(mul(hidden, down_w).astype(jnp.bfloat16))
    forward_out = (fwd_weight[0][:, None] * unpack_rows(own_sum, fwd_ids)).astype(jnp.bfloat16)

    share = gate_w.shape[0] // lax.axis_size("dp")
    first = lax.axis_index("dp") * share
    back_cols = lax.dynamic_slice_in_dim(back_all, first, share, 1)
    grad_cols = lax.dynamic_slice_in_dim(grad_all, first, share, 1)
    operands = (back_all, grad_all, back_cols, grad_cols, gate_w, up_w, down_w)
    tiles = [t for t in (384, 256, 128) if gate_w.shape[1] % t == 0]
    if tiles and back_all.shape[0] <= 512:
        gate_sum, up_sum, down_sum, partial = backward(*operands, tiles[0])
    else:
        gate_sum, up_sum, down_sum, partial = backward_plain(*operands)
    if lax.axis_size("et") == 2:
        partial = jnp.where(
            lax.axis_index("et") == 0, partial, jnp.concatenate([partial[CAP:], partial[:CAP]])
        )
    grad_rows = unpack_rows(scatter_et(partial), back_ids).astype(jnp.bfloat16)
    return (
        forward_out[None],
        grad_rows[None],
        gate_sum[None],
        up_sum[None],
        down_sum[None],
    )


def solution(mesh):
    rows3 = P("section", ("dp", "et"), None)
    rows2 = P("section", ("dp", "et"))
    columns = P("section", None, "et")
    return jax.shard_map(
        per_device,
        mesh=mesh,
        in_specs=(
            rows3, rows2, rows2, rows3, rows2, rows2, rows3,
            columns, columns, P("section", "et", None),
        ),
        out_specs=(
            rows3,
            rows3,
            P("section", "dp", "et"),
            P("section", "dp", "et"),
            P("section", "et", "dp"),
        ),
        check_vma=False,
    )
```

time: 976 us -> 162 us (0.17)
  waiting for transfers between devices: 825 us -> 61.5 us
  matrix products: 109 us -> 32.9 us
  Pallas kernels: 0 us -> 38.4 us
  blocking collectives: 24.2 us -> 0 us
    reduce_scatter x5 -> x0, waiting for transfers between devices: 825 us -> none  [the longest x1 280 us: backward_pass(): lax.psum_scatter(gate_term.astype(jnp.bfloat16), 'dp', scatter_dimension=...]
    dot_general x13 -> x5, matrix products: 104 us -> 29.4 us  [mul(): return lax.dot_general(a, b, dims, preferred_element_type=jnp.float32)]
    all_gather x0 -> x2, waiting for transfers between devices: none -> 46.7 us  [the longest x1 44.6 us: per_device(): grad_all = lax.all_gather(grad_packed, ('dp', 'et'), axis=0, tiled=True)]
    pallas_call x0 -> x1, Pallas kernels: none -> 38.4 us  [backward(): pl.pallas_call(functools.partial(back_kernel, own_rows), grid=(units // t...]
    all_gather x3 -> x0, blocking collectives: 24.2 us -> none  [the longest x1 8.22 us: per_device(): lax.all_gather(stash_packed, 'et', axis=0, tiled=True)]
    ppermute x2 -> x7, waiting for transfers between devices: 0.46 us -> 14.8 us  [passed_along(): lax.ppermute(block, axis, [((i - distance) % n, i) for i in range(n)])]
  transfers between devices with their start and end apart: 7 -> 9, of which waited for: 4 -> 7; matrix products, arithmetic and copies ran while one was open for 11% -> 21% of each run, Pallas kernels for 0% -> 24%
where the time goes in v1:
time: 162 us; the launch traced here: 161 us
  waiting for transfers between devices  61.5 us (38%)
  Pallas kernels  38.4 us (24%)
  matrix products  32.9 us (20%)
  between operations  14.2 us (9%)
  starting transfers between devices  6.52 us (4%)
  local copies, waits for them, and re-layouts  6.21 us (4%)
  other arithmetic  1.66 us (1%)
    all_gather x1, waiting for transfers between devices, per_device(): grad_all = lax.all_gather(grad_packed, ('dp', 'et'), axis=0, tiled=True)  44.6 us
    pallas_call x1, Pallas kernels, backward(): pl.pallas_call(functools.partial(back_kernel, own_rows), grid=(units // t...  38.4 us
    dot_general x5, matrix products, mul(): return lax.dot_general(a, b, dims, preferred_element_type=jnp.float32)  29.4 us
    ppermute x7, waiting for transfers between devices, passed_along(): lax.ppermute(block, axis, [((i - distance) % n, i) for i in range(n)])  14.8 us
    ppermute x7, starting transfers between devices, passed_along(): lax.ppermute(block, axis, [((i - distance) % n, i) for i in range(n)])  6.44 us
    unnamed x16, local copies, waits for them, and re-layouts  4.09 us
    dot_general x2, matrix products, unpack_rows(): jnp.dot(picker, packed, precision=lax.Precision.HIGHEST, preferred_elemen...  3.42 us
  transfers between devices with their start and end apart: 9, of which 7 were waited for; matrix products, arithmetic and copies ran while one was open for 21% of the time, Pallas kernels for 24%

profile of v1, /device:TPU:0, one launch (start us, length us, event | category | flops | bytes accessed | tf_op | source)
XLA Modules:
  0.0 161.3 jit_solution(1015731631076576362)
XLA Ops:
  7.2 1.1 copy-done
  8.3 1.6 convolution_convert_fusion.3
  10.5 2.0 %collective-permute-start = (s32[1,128]{1,0:T(1,128)}, s32[1,128]{1,0:T(1,128)S(1)}, u32[]{:S(2)}, u32[]{:S(2)}) collective-permute-start(s32[1,128]{1,0:T(1,128)} %param.11), channel_id=1, source_target_pairs={{2,0},{4,2},{6,4},{0,6},{3,1},{5,3},{7,5},{1,7},{10,8},{12,10},{14... | collective-permute-start | bytes 1544 | tf_op jit(solution)/shard_map/ppermute | solution.py:22
  12.4 0.8 select_reduce_fusion
  13.7 1.4 convolution_convert_fusion.2
  15.3 1.4 convolution_convert_fusion.4
  16.7 0.9 collective-permute-start.1
  17.6 1.0 collective-permute-done.5
  18.5 0.8 multiply_convert_fusion.1
  19.3 3.9 %collective-permute-done.1 = bf16[32,3072]{1,0:T(8,128)(2,1)S(1)} collective-permute-done((bf16[32,3072]{1,0:T(8,128)(2,1)S(1)}, bf16[32,3072]{1,0:T(8,128)(2,1)S(1)}, u32[]{:S(2)}, u32[]{:S(2)}) %collective-permute-start.1) | collective-permute-done | bytes 196640 | tf_op jit(solution)/shard_map/ppermute | solution.py:22
  23.2 1.5 collective-permute-start.2
  24.8 5.7 %collective-permute-done.2 = bf16[32,3072]{1,0:T(8,128)(2,1)S(1)} collective-permute-done((bf16[32,3072]{1,0:T(8,128)(2,1)S(1)}, bf16[32,3072]{1,0:T(8,128)(2,1)S(1)}, u32[]{:S(2)}, u32[]{:S(2)}) %collective-permute-start.2) | collective-permute-done | bytes 196640 | tf_op jit(solution)/shard_map/ppermute | solution.py:22
  30.5 8.6 %fusion.27 = f32[64,2688]{1,0:T(8,128)S(1)} fusion(bf16[64,3072]{1,0:T(8,128)(2,1)S(1)} %constant_dynamic-update-slice_fusion, bf16[1,3072,2688]{2,1,0:T(8,128)(2,1)} %param.17), kind=kOutput, calls=%fused_computation.42 | convolution fusion | flops 1056964608 | bytes 17596416 | tf_op jit(solution)/shard_map/dot_general | solution.py:17
  39.1 16.5 %convolution_convert_fusion.1 = bf16[64,3072]{1,0:T(8,128)(2,1)S(1)} fusion(f32[64,2688]{1,0:T(8,128)S(1)} %fusion.27, bf16[1,2688,3072]{2,1,0:T(8,128)(2,1)} %param.19, bf16[64,3072]{1,0:T(8,128)(2,1)S(1)} %constant_dynamic-update-slice_fusion, bf16[1,3072,2688]{2,1,0:T(8,128)(2,1)} %param.18), kind=kOutput, calls=%fused_computation.5 | convolution fusion | flops 2115158016 | bytes 34504704 | tf_op jit(solution)/shard_map/dot_general | solution.py:17
  56.4 2.1 %all-gather.3.cloned.1.call-done.back_ref = bf16[256,3072]{1,0:T(8,128)(2,1)} async-done(((bf16[32,3072]{1,0:T(8,128)(2,1)}), bf16[256,3072]{1,0:T(8,128)(2,1)}) %all-gather.3.cloned.1.call-update) | async-done | bytes 1572880 | tf_op jit(solution)/shard_map/all_gather | solution.py:189
  58.4 1.0 constant_dynamic-slice_fusion.1
  59.6 44.6 %all-gather.5.cloned.1.call-done.grad_ref = bf16[256,3072]{1,0:T(8,128)(2,1)} async-done(((bf16[32,3072]{1,0:T(8,128)(2,1)}), bf16[256,3072]{1,0:T(8,128)(2,1)}) %all-gather.5.cloned.1.call-update) | async-done | bytes 1572880 | tf_op jit(solution)/shard_map/all_gather | solution.py:193
  104.2 1.0 constant_dynamic-slice_fusion.grad_cols
  105.2 1.4 copy-done.2
  106.6 1.4 copy-done.3
  108.1 38.4 %shard_map.137 = (bf16[768,2688]{1,0:T(8,128)(2,1)}, bf16[768,2688]{1,0:T(8,128)(2,1)}, bf16[2688,768]{1,0:T(8,128)(2,1)}, bf16[64,3072]{1,0:T(8,128)(2,1)S(1)}) custom-call(bf16[256,3072]{1,0:T(8,128)(2,1)S(1)} %copy-done.2, bf16[256,3072]{1,0:T(8,128)(2,1)S(1)} %copy-done.3, bf16[768,256]{1,0:T(8,128)(2,1)S(1)} %bitcast.38, ...), custom_call_target="tpu_custom_call" | custom-call | flops 17968398336 | bytes 68222976 | tf_op jit(solution)/shard_map/pallas_call | solution.py:119
  147.3 1.7 %fusion.2 = bf16[1,128,3072]{2,1,0:T(8,128)(2,1)} fusion(f32[128]{0:T(128)S(1)} %bitcast.47, bf16[32,3072]{1,0:T(8,128)(2,1)S(1)} %collective-permute-done.3, bf16[64,3072]{1,0:T(8,128)(2,1)S(1)} %convolution_convert_fusion.1, s32[128]{0:T(128)S(1)} %bitcast.48), kind=kOutput, calls=%fused_computation.4 | convolution fusion | flops 152080384 | bytes 1180672 | tf_op jit(solution)/shard_map/dot_general | solution.py:39
  149.0 3.7 %collective-permute-done.6 = bf16[32,3072]{1,0:T(8,128)(2,1)S(1)} collective-permute-done((bf16[32,3072]{1,0:T(8,128)(2,1)S(1)}, bf16[32,3072]{1,0:T(8,128)(2,1)S(1)}, u32[]{:S(2)}, u32[]{:S(2)}) %collective-permute-start.6) | collective-permute-done | bytes 196640 | tf_op jit(solution)/shard_map/ppermute | solution.py:22
  152.7 1.7 %fusion.1 = bf16[1,128,3072]{2,1,0:T(8,128)(2,1)} fusion(bf16[32,3072]{1,0:T(8,128)(2,1)S(1)} %collective-permute-done.6, bf16[64,3072]{1,0:T(8,128)(2,1)S(1)} %maximum_select_fusion, s32[128]{0:T(128)S(1)} %bitcast.44), kind=kOutput, calls=%fused_computation.3 | convolution fusion | flops 151687168 | bytes 1180160 | tf_op jit(solution)/shard_map/dot_general | solution.py:39
  (29 shorter events, 3.1 us)
Async XLA Ops:
  7.2 1.1 copy-start
  7.2 51.2 %all-gather.3.cloned.1.call-start = ((), (), s32[]{:S(2)}) async-start(), calls=%async_computation | async-start | bytes 1769472 | tf_op jit(solution)/shard_map/all_gather | solution.py:189
  9.9 94.3 %all-gather.5.cloned.1.call-start = ((), (), s32[]{:S(2)}) async-start(), calls=%async_computation.1 | async-start | bytes 1769472 | tf_op jit(solution)/shard_map/all_gather | solution.py:193
  9.9 3.8 %collective-permute-start.4 = (s32[1,128]{1,0:T(1,128)}, s32[1,128]{1,0:T(1,128)S(1)}, u32[]{:S(2)}, u32[]{:S(2)}) collective-permute-start(s32[1,128]{1,0:T(1,128)} %param.14), channel_id=1, source_target_pairs={{6,0},{0,2},{2,4},{4,6},{7,1},{1,3},{3,5},{5,7},{14,8},{8,10},{10,... | collective-permute-start | bytes 1544 | tf_op jit(solution)/shard_map/ppermute | solution.py:22
  10.5 4.9 %collective-permute-start = (s32[1,128]{1,0:T(1,128)}, s32[1,128]{1,0:T(1,128)S(1)}, u32[]{:S(2)}, u32[]{:S(2)}) collective-permute-start(s32[1,128]{1,0:T(1,128)} %param.11), channel_id=1, source_target_pairs={{2,0},{4,2},{6,4},{0,6},{3,1},{5,3},{7,5},{1,7},{10,8},{12,10},{14... | collective-permute-start | bytes 1544 | tf_op jit(solution)/shard_map/ppermute | solution.py:22
  15.1 3.4 %collective-permute-start.5 = (bf16[32,3072]{1,0:T(8,128)(2,1)S(1)}, bf16[32,3072]{1,0:T(8,128)(2,1)S(1)}, u32[]{:S(2)}, u32[]{:S(2)}) collective-permute-start(bf16[32,3072]{1,0:T(8,128)(2,1)S(1)} %convolution_convert_fusion.2), channel_id=1, source_target_pairs={{2,0},{4,2},{6,4},{0,6},{3,1},{5,3},{7,5},{1,7},{10,8},{12,10},{14... | collective-permute-start | bytes 589832 | tf_op jit(solution)/shard_map/ppermute | solution.py:22
  16.7 6.5 %collective-permute-start.1 = (bf16[32,3072]{1,0:T(8,128)(2,1)S(1)}, bf16[32,3072]{1,0:T(8,128)(2,1)S(1)}, u32[]{:S(2)}, u32[]{:S(2)}) collective-permute-start(bf16[32,3072]{1,0:T(8,128)(2,1)S(1)} %convolution_convert_fusion.4), channel_id=1, source_target_pairs={{6,0},{0,2},{2,4},{4,6},{7,1},{1,3},{3,5},{5,7},{14,8},{8,10},{10,... | collective-permute-start | bytes 589832 | tf_op jit(solution)/shard_map/ppermute | solution.py:22
  23.2 7.2 %collective-permute-start.2 = (bf16[32,3072]{1,0:T(8,128)(2,1)S(1)}, bf16[32,3072]{1,0:T(8,128)(2,1)S(1)}, u32[]{:S(2)}, u32[]{:S(2)}) collective-permute-start(bf16[32,3072]{1,0:T(8,128)(2,1)S(1)} %collective-permute-done.1), channel_id=1, source_target_pairs={{1,0},{0,1},{3,2},{2,3},{5,4},{4,5},{7,6},{6,7},{9,8},{8,9},{11,10... | collective-permute-start | bytes 589832 | tf_op jit(solution)/shard_map/ppermute | solution.py:22
  55.6 91.6 %collective-permute-start.3 = (bf16[32,3072]{1,0:T(8,128)(2,1)S(1)}, bf16[32,3072]{1,0:T(8,128)(2,1)S(1)}, u32[]{:S(2)}, u32[]{:S(2)}) collective-permute-start(bf16[32,3072]{1,0:T(8,128)(2,1)S(1)} %slice.25), channel_id=1, source_target_pairs={{1,0},{0,1},{3,2},{2,3},{5,4},{4,5},{7,6},{6,7},{9,8},{8,9},{11,10... | collective-permute-start | bytes 589832 | tf_op jit(solution)/shard_map/ppermute | solution.py:22
  105.2 1.4 copy-start.2
  106.6 1.4 copy-start.3
  108.0 39.2 %copy-start.5 = (f32[1,128]{1,0:T(1,128)S(1)}, f32[1,128]{1,0:T(1,128)}, u32[]{:S(2)}) copy-start(f32[1,128]{1,0:T(1,128)} %param.12) | copy-start | bytes 1540
  108.0 39.2 %copy-start.6 = (s32[1,128]{1,0:T(1,128)S(1)}, s32[1,128]{1,0:T(1,128)}, u32[]{:S(2)}) copy-start(s32[1,128]{1,0:T(1,128)} %param.11) | copy-start | bytes 1540
  108.1 44.7 %copy-start.4 = (s32[1,128]{1,0:T(1,128)S(1)}, s32[1,128]{1,0:T(1,128)}, u32[]{:S(2)}) copy-start(s32[1,128]{1,0:T(1,128)} %param.14) | copy-start | bytes 1540
  108.1 46.4 %copy-start.1 = (bf16[1,128,3072]{2,1,0:T(8,128)(2,1)S(1)}, bf16[1,128,3072]{2,1,0:T(8,128)(2,1)}, u32[]{:S(2)}) copy-start(bf16[1,128,3072]{2,1,0:T(8,128)(2,1)} %param.13) | copy-start | bytes 2359300
  146.6 6.1 %collective-permute-start.6 = (bf16[32,3072]{1,0:T(8,128)(2,1)S(1)}, bf16[32,3072]{1,0:T(8,128)(2,1)S(1)}, u32[]{:S(2)}, u32[]{:S(2)}) collective-permute-start(bf16[32,3072]{1,0:T(8,128)(2,1)S(1)} %slice.27), channel_id=1, source_target_pairs={{1,0},{0,1},{3,2},{2,3},{5,4},{4,5},{7,6},{6,7},{9,8},{8,9},{11,10... | collective-permute-start | bytes 589832 | tf_op jit(solution)/shard_map/ppermute | solution.py:22
Sparse Core Ops, SparseCore 0:
  10.8 47.6 all-gather.2
  61.2 42.9 all-gather.4

commit v2 on v1

--- a/solution.py
+++ b/solution.py
@@ -52,6 +52,15 @@
         other = passed_along(partial[CAP:], "et", 1)
         return partial[:CAP].astype(jnp.float32) + other.astype(jnp.float32)
     return lax.psum_scatter(partial, "et", scatter_dimension=0, tiled=True).astype(jnp.float32)
+
+
+def gather_replicas(rows):
+    if lax.axis_size("et") == 2:
+        blocks = [rows] + [passed_along(rows, "dp", d) for d in range(1, lax.axis_size("dp"))]
+        pairs = [piece for block in blocks for piece in (block, passed_along(block, "et", 1))]
+        return pairs, 0
+    own = lax.axis_index("dp") * lax.axis_size("et") * rows.shape[0]
+    return [lax.all_gather(rows, ("dp", "et"), axis=0, tiled=True)], own
 
 
 def gates(pre_gate, pre_up, grad_hidden):
@@ -67,7 +76,7 @@
     own_rows,
     back_ref,
     grad_ref,
-    back_cols_t,
+    back_cols,
     grad_cols,
     gate_ref,
     up_ref,
@@ -76,22 +85,24 @@
     up_out,
     down_out,
     rows_out,
-    gate_act,
-    up_act,
     total,
+    back_cols_t,
 ):
     step = pl.program_id(0)
+
+    @pl.when(step == 0)
+    def _():
+        back_cols_t[...] = back_cols[...].T
+
     pre_gate = mul(back_ref[...], gate_ref[...])
     pre_up = mul(back_ref[...], up_ref[...])
     grad_hidden = mul(grad_ref[...], down_ref[...], NT)
     hidden, grad_gate, grad_up = gates(pre_gate, pre_up, grad_hidden)
-    gate_act[...] = grad_gate
-    up_act[...] = grad_up
     gate_out[...] = mul(back_cols_t[...], grad_gate).astype(jnp.bfloat16)
     up_out[...] = mul(back_cols_t[...], grad_up).astype(jnp.bfloat16)
     down_out[...] = mul(hidden, grad_cols[...], TN).astype(jnp.bfloat16)
-    own = pl.ds(pl.multiple_of(lax.axis_index("dp") * own_rows, own_rows), own_rows)
-    term = mul(gate_act[own, :], gate_ref[...], NT) + mul(up_act[own, :], up_ref[...], NT)
+    term = mul(grad_gate[:own_rows], gate_ref[...], NT)
+    term += mul(grad_up[:own_rows], up_ref[...], NT)
 
     @pl.when(step == 0)
     def _():
@@ -122,7 +133,7 @@
         in_specs=[
             once((rows, depth)),
             once((rows, depth)),
-            once((share, rows)),
+            once((rows, share)),
             once((rows, share)),
             pl.BlockSpec((depth, tile), across),
             pl.BlockSpec((depth, tile), across),
@@ -141,9 +152,8 @@
             jax.ShapeDtypeStruct((own_rows, depth), jnp.bfloat16),
         ],
         scratch_shapes=[
-            pltpu.VMEM((rows, tile), jnp.bfloat16),
-            pltpu.VMEM((rows, tile), jnp.bfloat16),
             pltpu.VMEM((own_rows, depth), jnp.float32),
+            pltpu.VMEM((share, rows), jnp.bfloat16),
         ],
         compiler_params=pltpu.CompilerParams(vmem_limit_bytes=48 * 2**20),
         cost_estimate=pl.CostEstimate(
@@ -151,14 +161,13 @@
             bytes_accessed=6 * units * (depth + share) + 8 * rows * depth,
             transcendentals=rows * units,
         ),
-    )(back_all, grad_all, back_cols.T, grad_cols, gate_w, up_w, down_w)
-
-
-def backward_plain(back_all, grad_all, back_cols, grad_cols, gate_w, up_w, down_w):
+    )(back_all, grad_all, back_cols, grad_cols, gate_w, up_w, down_w)
+
+
+def backward_plain(back_all, grad_all, back_cols, grad_cols, gate_w, up_w, down_w, start):
     pre_gate, pre_up = mul(back_all, gate_w), mul(back_all, up_w)
     hidden, grad_gate, grad_up = gates(pre_gate, pre_up, mul(grad_all, down_w, NT))
     own_rows = back_all.shape[0] // lax.axis_size("dp")
-    start = lax.axis_index("dp") * own_rows
     own_gate = lax.dynamic_slice_in_dim(grad_gate, start, own_rows, 0)
     own_up = lax.dynamic_slice_in_dim(grad_up, start, own_rows, 0)
     return (
@@ -186,34 +195,36 @@
     back_ids_there = passed_along(back_slot, "section", 1)[0]
     fwd_ids_there = passed_along(fwd_slot, "section", -1)[0]
     stash_packed = pack_rows(stashed[0], back_ids)
-    back_all = lax.all_gather(stash_packed, ("dp", "et"), axis=0, tiled=True)
+    back_pieces, own = gather_replicas(stash_packed)
     returned = passed_along(pack_rows(grad_handoff[0], back_ids_there), "section", -1)
     weights = pack_values(back_weight[0], back_ids)
     grad_packed = (weights[:, None] * returned.astype(jnp.float32)).astype(jnp.bfloat16)
-    grad_all = lax.all_gather(grad_packed, ("dp", "et"), axis=0, tiled=True)
+    grad_pieces = gather_replicas(grad_packed)[0]
 
     arrived = passed_along(pack_rows(handoff[0], fwd_ids_there), "section", 1)
     fwd_rows = gather_et(arrived)
     pre_gate = mul(fwd_rows, gate_w)
     pre_up = mul(fwd_rows, up_w)
     hidden = (pre_gate * jax.nn.sigmoid(pre_gate) * pre_up).astype(jnp.bfloat16)
-    own_sum = scatter_et(mul(hidden, down_w).astype(jnp.bfloat16))
+    fwd_partial = mul(hidden, down_w).astype(jnp.bfloat16)
+    fwd_partial, back_pieces, grad_pieces = lax.optimization_barrier(
+        (fwd_partial, back_pieces, grad_pieces)
+    )
+    own_sum = scatter_et(fwd_partial)
     forward_out = (fwd_weight[0][:, None] * unpack_rows(own_sum, fwd_ids)).astype(jnp.bfloat16)
 
+    back_all = jnp.concatenate(back_pieces, axis=0)
+    grad_all = jnp.concatenate(grad_pieces, axis=0)
     share = gate_w.shape[0] // lax.axis_size("dp")
     first = lax.axis_index("dp") * share
     back_cols = lax.dynamic_slice_in_dim(back_all, first, share, 1)
     grad_cols = lax.dynamic_slice_in_dim(grad_all, first, share, 1)
     operands = (back_all, grad_all, back_cols, grad_cols, gate_w, up_w, down_w)
     tiles = [t for t in (384, 256, 128) if gate_w.shape[1] % t == 0]
-    if tiles and back_all.shape[0] <= 512:
+    if tiles and lax.axis_size("et") == 2 and back_all.shape[0] <= 512:
         gate_sum, up_sum, down_sum, partial = backward(*operands, tiles[0])
     else:
-        gate_sum, up_sum, down_sum, partial = backward_plain(*operands)
-    if lax.axis_size("et") == 2:
-        partial = jnp.where(
-            lax.axis_index("et") == 0, partial, jnp.concatenate([partial[CAP:], partial[:CAP]])
-        )
+        gate_sum, up_sum, down_sum, partial = backward_plain(*operands, own)
     grad_rows = unpack_rows(scatter_et(partial), back_ids).astype(jnp.bfloat16)
     return (
         forward_out[None],

time: 162 us -> 131 us (0.81)
  waiting for transfers between devices: 61.5 us -> 24.1 us
  starting transfers between devices: 6.52 us -> 28.4 us
  between operations: 14.2 us -> 0.92 us
  matrix products: 32.9 us -> 30.8 us
    all_gather x2 -> x0, waiting for transfers between devices: 46.7 us -> none  [the longest x1 44.6 us: per_device(): grad_all = lax.all_gather(grad_packed, ('dp', 'et'), axis=0, tiled=True)]
    ppermute x7 -> x21, starting transfers between devices: 6.44 us -> 28.4 us  [passed_along(): lax.ppermute(block, axis, [((i - distance) % n, i) for i in range(n)])]
    ppermute x7 -> x21, waiting for transfers between devices: 14.8 us -> 24.1 us  [passed_along(): lax.ppermute(block, axis, [((i - distance) % n, i) for i in range(n)])]
    dot_general x5, matrix products: 29.4 us -> 27.3 us  [mul(): return lax.dot_general(a, b, dims, preferred_element_type=jnp.float32)]
    unnamed x16 -> x29, local copies, waits for them, and re-layouts: 4.09 us -> 4.79 us
  transfers between devices with their start and end apart: 9 -> 21, of which waited for: 7 -> 5; matrix products, arithmetic and copies ran while one was open for 21% -> 23% of each run, Pallas kernels for 24% -> 0%
where the time goes in v2:
time: 131 us; the launch traced here: 129 us
  Pallas kernels  38.5 us (29%)
  matrix products  30.8 us (24%)
  starting transfers between devices  28.4 us (22%)
  waiting for transfers between devices  24.1 us (18%)
  local copies, waits for them, and re-layouts  5.97 us (5%)
    pallas_call x1, Pallas kernels, backward(): pl.pallas_call(functools.partial(back_kernel, own_rows), grid=(units // t...  38.5 us
    ppermute x21, starting transfers between devices, passed_along(): lax.ppermute(block, axis, [((i - distance) % n, i) for i in range(n)])  28.4 us
    dot_general x5, matrix products, mul(): return lax.dot_general(a, b, dims, preferred_element_type=jnp.float32)  27.3 us
    ppermute x21, waiting for transfers between devices, passed_along(): lax.ppermute(block, axis, [((i - distance) % n, i) for i in range(n)])  24.1 us
    unnamed x29, local copies, waits for them, and re-layouts  4.79 us
    dot_general x2, matrix products, unpack_rows(): jnp.dot(picker, packed, precision=lax.Precision.HIGHEST, preferred_elemen...  3.42 us
  transfers between devices with their start and end apart: 21, of which 5 were waited for; matrix products, arithmetic and copies ran while one was open for 23% of the time, Pallas kernels for 0%

profile of v2, /device:TPU:0, one launch (start us, length us, event | category | flops | bytes accessed | tf_op | source)
XLA Modules:
  0.0 128.9 jit_solution(13693859673787174638)
XLA Ops:
  2.9 3.1 %collective-permute-start.4 = (bf16[32,3072]{1,0:T(8,128)(2,1)S(1)}, bf16[32,3072]{1,0:T(8,128)(2,1)S(1)}, u32[]{:S(2)}, u32[]{:S(2)}) collective-permute-start(bf16[32,3072]{1,0:T(8,128)(2,1)S(1)} %convolution_convert_fusion.3), channel_id=1, source_target_pairs={{24,0},{0,8},{8,16},{16,24},{25,1},{1,9},{9,17},{17,25},{26,2},{2,... | collective-permute-start | bytes 589832 | tf_op jit(solution)/shard_map/ppermute | solution.py:22
  6.0 2.6 %collective-permute-start.6 = (bf16[32,3072]{1,0:T(8,128)(2,1)S(1)}, bf16[32,3072]{1,0:T(8,128)(2,1)S(1)}, u32[]{:S(2)}, u32[]{:S(2)}) collective-permute-start(bf16[32,3072]{1,0:T(8,128)(2,1)S(1)} %convolution_convert_fusion.3), channel_id=1, source_target_pairs={{16,0},{24,8},{0,16},{8,24},{17,1},{25,9},{1,17},{9,25},{18,2},{26... | collective-permute-start | bytes 589832 | tf_op jit(solution)/shard_map/ppermute | solution.py:22
  8.9 1.4 %convolution_convert_fusion.2 = bf16[32,3072]{1,0:T(8,128)(2,1)S(1)} fusion(bf16[1,128,3072]{2,1,0:T(8,128)(2,1)} %param.16, s32[128]{0:T(128)S(1)} %bitcast.43), kind=kOutput, calls=%fused_computation.6 | convolution fusion | flops 25268224 | bytes 983552 | tf_op jit(solution)/shard_map/dot_general | solution.py:17
  10.3 1.3 collective-permute-start.11
  12.1 1.4 %collective-permute-start.8 = (bf16[32,3072]{1,0:T(8,128)(2,1)S(1)}, bf16[32,3072]{1,0:T(8,128)(2,1)S(1)}, u32[]{:S(2)}, u32[]{:S(2)}) collective-permute-start(bf16[32,3072]{1,0:T(8,128)(2,1)S(1)} %convolution_convert_fusion.3), channel_id=1, source_target_pairs={{8,0},{16,8},{24,16},{0,24},{9,1},{17,9},{25,17},{1,25},{10,2},{18... | collective-permute-start | bytes 589832 | tf_op jit(solution)/shard_map/ppermute | solution.py:22
  13.9 1.7 %collective-permute-start.3 = (bf16[32,3072]{1,0:T(8,128)(2,1)S(1)}, bf16[32,3072]{1,0:T(8,128)(2,1)S(1)}, u32[]{:S(2)}, u32[]{:S(2)}) collective-permute-start(bf16[32,3072]{1,0:T(8,128)(2,1)S(1)} %convolution_convert_fusion.3), channel_id=1, source_target_pairs={{1,0},{0,1},{3,2},{2,3},{5,4},{4,5},{7,6},{6,7},{9,8},{8,9},{11,10... | collective-permute-start | bytes 589832 | tf_op jit(solution)/shard_map/ppermute | solution.py:22
  15.5 6.4 %collective-permute-done.6 = bf16[32,3072]{1,0:T(8,128)(2,1)S(1)} collective-permute-done((bf16[32,3072]{1,0:T(8,128)(2,1)S(1)}, bf16[32,3072]{1,0:T(8,128)(2,1)S(1)}, u32[]{:S(2)}, u32[]{:S(2)}) %collective-permute-start.6) | collective-permute-done | bytes 196640 | tf_op jit(solution)/shard_map/ppermute | solution.py:22
  22.0 1.5 %collective-permute-start.5 = (bf16[32,3072]{1,0:T(8,128)(2,1)S(1)}, bf16[32,3072]{1,0:T(8,128)(2,1)S(1)}, u32[]{:S(2)}, u32[]{:S(2)}) collective-permute-start(bf16[32,3072]{1,0:T(8,128)(2,1)S(1)} %collective-permute-done.4), channel_id=1, source_target_pairs={{1,0},{0,1},{3,2},{2,3},{5,4},{4,5},{7,6},{6,7},{9,8},{8,9},{11,10... | collective-permute-start | bytes 589832 | tf_op jit(solution)/shard_map/ppermute | solution.py:22
  24.0 1.5 %collective-permute-start.2 = (bf16[32,3072]{1,0:T(8,128)(2,1)S(1)}, bf16[32,3072]{1,0:T(8,128)(2,1)S(1)}, u32[]{:S(2)}, u32[]{:S(2)}) collective-permute-start(bf16[32,3072]{1,0:T(8,128)(2,1)S(1)} %collective-permute-done.1), channel_id=1, source_target_pairs={{1,0},{0,1},{3,2},{2,3},{5,4},{4,5},{7,6},{6,7},{9,8},{8,9},{11,10... | collective-permute-start | bytes 589832 | tf_op jit(solution)/shard_map/ppermute | solution.py:22
  25.7 11.5 %collective-permute-done.2 = bf16[32,3072]{1,0:T(8,128)(2,1)S(1)} collective-permute-done((bf16[32,3072]{1,0:T(8,128)(2,1)S(1)}, bf16[32,3072]{1,0:T(8,128)(2,1)S(1)}, u32[]{:S(2)}, u32[]{:S(2)}) %collective-permute-start.2) | collective-permute-done | bytes 196640 | tf_op jit(solution)/shard_map/ppermute | solution.py:22
  37.2 2.5 %collective-permute-start.13 = (bf16[32,3072]{1,0:T(8,128)(2,1)S(1)}, bf16[32,3072]{1,0:T(8,128)(2,1)S(1)}, u32[]{:S(2)}, u32[]{:S(2)}) collective-permute-start(bf16[32,3072]{1,0:T(8,128)(2,1)S(1)} %multiply_convert_fusion.1), channel_id=1, source_target_pairs={{24,0},{0,8},{8,16},{16,24},{25,1},{1,9},{9,17},{17,25},{26,2},{2,... | collective-permute-start | bytes 589832 | tf_op jit(solution)/shard_map/ppermute | solution.py:22
  39.7 3.4 %collective-permute-start.15 = (bf16[32,3072]{1,0:T(8,128)(2,1)S(1)}, bf16[32,3072]{1,0:T(8,128)(2,1)S(1)}, u32[]{:S(2)}, u32[]{:S(2)}) collective-permute-start(bf16[32,3072]{1,0:T(8,128)(2,1)S(1)} %multiply_convert_fusion.1), channel_id=1, source_target_pairs={{16,0},{24,8},{0,16},{8,24},{17,1},{25,9},{1,17},{9,25},{18,2},{26... | collective-permute-start | bytes 589832 | tf_op jit(solution)/shard_map/ppermute | solution.py:22
  43.1 8.6 %fusion.27 = f32[64,2688]{1,0:T(8,128)S(1)} fusion(bf16[64,3072]{1,0:T(8,128)(2,1)S(1)} %constant_dynamic-update-slice_fusion, bf16[1,3072,2688]{2,1,0:T(8,128)(2,1)} %param.17), kind=kOutput, calls=%fused_computation.57 | convolution fusion | flops 1056964608 | bytes 17596416 | tf_op jit(solution)/shard_map/dot_general | solution.py:17
  51.8 1.6 %collective-permute-start.9 = (bf16[32,3072]{1,0:T(8,128)(2,1)S(1)}, bf16[32,3072]{1,0:T(8,128)(2,1)}, u32[]{:S(2)}, u32[]{:S(2)}) collective-permute-start(bf16[32,3072]{1,0:T(8,128)(2,1)S(1)} %collective-permute-done.8), channel_id=1, source_target_pairs={{1,0},{0,1},{3,2},{2,3},{5,4},{4,5},{7,6},{6,7},{9,8},{8,9},{11,10... | collective-permute-start | bytes 589832 | tf_op jit(solution)/shard_map/ppermute | solution.py:22
  53.9 1.5 %collective-permute-start.14 = (bf16[32,3072]{1,0:T(8,128)(2,1)S(1)}, bf16[32,3072]{1,0:T(8,128)(2,1)}, u32[]{:S(2)}, u32[]{:S(2)}) collective-permute-start(bf16[32,3072]{1,0:T(8,128)(2,1)S(1)} %collective-permute-done.13), channel_id=1, source_target_pairs={{1,0},{0,1},{3,2},{2,3},{5,4},{4,5},{7,6},{6,7},{9,8},{8,9},{11,10... | collective-permute-start | bytes 589832 | tf_op jit(solution)/shard_map/ppermute | solution.py:22
  56.2 1.2 collective-permute-start.18
  57.4 16.2 %convolution_convert_fusion.1 = bf16[64,3072]{1,0:T(8,128)(2,1)S(1)} fusion(f32[64,2688]{1,0:T(8,128)S(1)} %fusion.27, bf16[1,2688,3072]{2,1,0:T(8,128)(2,1)} %param.19, bf16[64,3072]{1,0:T(8,128)(2,1)S(1)} %constant_dynamic-update-slice_fusion, bf16[1,3072,2688]{2,1,0:T(8,128)(2,1)} %param.18), kind=kOutput, calls=%fused_computation.5 | convolution fusion | flops 2115158016 | bytes 34504704 | tf_op jit(solution)/shard_map/dot_general | solution.py:17
  73.8 0.9 constant_dynamic-update-slice_fusion.16
  77.7 1.0 constant_dynamic-update-slice_fusion.2
  78.9 38.5 %shard_map.137 = (bf16[768,2688]{1,0:T(8,128)(2,1)}, bf16[768,2688]{1,0:T(8,128)(2,1)}, bf16[2688,768]{1,0:T(8,128)(2,1)}, bf16[64,3072]{1,0:T(8,128)(2,1)S(1)}) custom-call(bf16[256,3072]{1,0:T(8,128)(2,1)S(1)} %get-tuple-element.47.back_ref, bf16[256,3072]{1,0:T(8,128)(2,1)S(1)} %get-tuple-element.48.grad_ref, ...), custom_call_target="tpu_custom_call" | custom-call | flops 17968398336 | bytes 68222976 | tf_op jit(solution)/shard_map/pallas_call | solution.py:130
  117.4 1.5 %collective-permute-start.20 = (bf16[32,3072]{1,0:T(8,128)(2,1)S(1)}, bf16[32,3072]{1,0:T(8,128)(2,1)S(1)}, u32[]{:S(2)}, u32[]{:S(2)}) collective-permute-start(bf16[32,3072]{1,0:T(8,128)(2,1)S(1)} %slice.15), channel_id=1, source_target_pairs={{1,0},{0,1},{3,2},{2,3},{5,4},{4,5},{7,6},{6,7},{9,8},{8,9},{11,10... | collective-permute-start | bytes 589832 | tf_op jit(solution)/shard_map/ppermute | solution.py:22
  119.6 5.5 %collective-permute-done.20 = bf16[32,3072]{1,0:T(8,128)(2,1)S(1)} collective-permute-done((bf16[32,3072]{1,0:T(8,128)(2,1)S(1)}, bf16[32,3072]{1,0:T(8,128)(2,1)S(1)}, u32[]{:S(2)}, u32[]{:S(2)}) %collective-permute-start.20) | collective-permute-done | bytes 196640 | tf_op jit(solution)/shard_map/ppermute | solution.py:22
  125.1 1.7 %fusion.1 = bf16[1,128,3072]{2,1,0:T(8,128)(2,1)} fusion(bf16[32,3072]{1,0:T(8,128)(2,1)S(1)} %collective-permute-done.20, bf16[64,3072]{1,0:T(8,128)(2,1)S(1)} %get-tuple-element.43, s32[128]{0:T(128)S(1)} %bitcast.42), kind=kOutput, calls=%fused_computation.3 | convolution fusion | flops 151687168 | bytes 1180160 | tf_op jit(solution)/shard_map/dot_general | solution.py:39
  127.2 1.7 %fusion.2 = bf16[1,128,3072]{2,1,0:T(8,128)(2,1)} fusion(f32[128]{0:T(128)S(1)} %bitcast.45, bf16[32,3072]{1,0:T(8,128)(2,1)S(1)} %collective-permute-done.19, bf16[64,3072]{1,0:T(8,128)(2,1)S(1)} %convolution_convert_fusion.1, s32[128]{0:T(128)S(1)} %bitcast.46), kind=kOutput, calls=%fused_computation.4 | convolution fusion | flops 152080384 | bytes 1180672 | tf_op jit(solution)/shard_map/dot_general | solution.py:39
  (63 shorter events, 9.6 us)
Async XLA Ops:
  0.6 12.8 %copy-start.3 = (s32[1,128]{1,0:T(1,128)S(1)}, s32[1,128]{1,0:T(1,128)}, u32[]{:S(2)}) copy-start(s32[1,128]{1,0:T(1,128)} %param.14) | copy-start | bytes 1540
  0.7 12.8 %copy-start.6 = (f32[1,128]{1,0:T(1,128)S(1)}, f32[1,128]{1,0:T(1,128)}, u32[]{:S(2)}) copy-start(f32[1,128]{1,0:T(1,128)} %param.15) | copy-start | bytes 1540
  0.7 8.3 %collective-permute-start.10 = (s32[1,128]{1,0:T(1,128)}, s32[1,128]{1,0:T(1,128)S(1)}, u32[]{:S(2)}, u32[]{:S(2)}) collective-permute-start(s32[1,128]{1,0:T(1,128)} %param.14), channel_id=1, source_target_pairs={{6,0},{0,2},{2,4},{4,6},{7,1},{1,3},{3,5},{5,7},{14,8},{8,10},{10,... | collective-permute-start | bytes 1544 | tf_op jit(solution)/shard_map/ppermute | solution.py:22
  2.9 11.0 %collective-permute-start.4 = (bf16[32,3072]{1,0:T(8,128)(2,1)S(1)}, bf16[32,3072]{1,0:T(8,128)(2,1)S(1)}, u32[]{:S(2)}, u32[]{:S(2)}) collective-permute-start(bf16[32,3072]{1,0:T(8,128)(2,1)S(1)} %convolution_convert_fusion.3), channel_id=1, source_target_pairs={{24,0},{0,8},{8,16},{16,24},{25,1},{1,9},{9,17},{17,25},{26,2},{2,... | collective-permute-start | bytes 589832 | tf_op jit(solution)/shard_map/ppermute | solution.py:22
  6.0 16.0 %collective-permute-start.6 = (bf16[32,3072]{1,0:T(8,128)(2,1)S(1)}, bf16[32,3072]{1,0:T(8,128)(2,1)S(1)}, u32[]{:S(2)}, u32[]{:S(2)}) collective-permute-start(bf16[32,3072]{1,0:T(8,128)(2,1)S(1)} %convolution_convert_fusion.3), channel_id=1, source_target_pairs={{16,0},{24,8},{0,16},{8,24},{17,1},{25,9},{1,17},{9,25},{18,2},{26... | collective-permute-start | bytes 589832 | tf_op jit(solution)/shard_map/ppermute | solution.py:22
  8.6 3.0 %collective-permute-start = (s32[1,128]{1,0:T(1,128)}, s32[1,128]{1,0:T(1,128)S(1)}, u32[]{:S(2)}, u32[]{:S(2)}) collective-permute-start(s32[1,128]{1,0:T(1,128)} %param.11), channel_id=1, source_target_pairs={{2,0},{4,2},{6,4},{0,6},{3,1},{5,3},{7,5},{1,7},{10,8},{12,10},{14... | collective-permute-start | bytes 1544 | tf_op jit(solution)/shard_map/ppermute | solution.py:22
  10.3 13.2 %collective-permute-start.11 = (bf16[32,3072]{1,0:T(8,128)(2,1)S(1)}, bf16[32,3072]{1,0:T(8,128)(2,1)S(1)}, u32[]{:S(2)}, u32[]{:S(2)}) collective-permute-start(bf16[32,3072]{1,0:T(8,128)(2,1)S(1)} %convolution_convert_fusion.2), channel_id=1, source_target_pairs={{2,0},{4,2},{6,4},{0,6},{3,1},{5,3},{7,5},{1,7},{10,8},{12,10},{14... | collective-permute-start | bytes 589832 | tf_op jit(solution)/shard_map/ppermute | solution.py:22
  11.8 12.2 %collective-permute-start.1 = (bf16[32,3072]{1,0:T(8,128)(2,1)S(1)}, bf16[32,3072]{1,0:T(8,128)(2,1)S(1)}, u32[]{:S(2)}, u32[]{:S(2)}) collective-permute-start(bf16[32,3072]{1,0:T(8,128)(2,1)S(1)} %convolution_convert_fusion.4), channel_id=1, source_target_pairs={{6,0},{0,2},{2,4},{4,6},{7,1},{1,3},{3,5},{5,7},{14,8},{8,10},{10,... | collective-permute-start | bytes 589832 | tf_op jit(solution)/shard_map/ppermute | solution.py:22
  12.1 27.6 %collective-permute-start.8 = (bf16[32,3072]{1,0:T(8,128)(2,1)S(1)}, bf16[32,3072]{1,0:T(8,128)(2,1)S(1)}, u32[]{:S(2)}, u32[]{:S(2)}) collective-permute-start(bf16[32,3072]{1,0:T(8,128)(2,1)S(1)} %convolution_convert_fusion.3), channel_id=1, source_target_pairs={{8,0},{16,8},{24,16},{0,24},{9,1},{17,9},{25,17},{1,25},{10,2},{18... | collective-permute-start | bytes 589832 | tf_op jit(solution)/shard_map/ppermute | solution.py:22
  13.9 29.3 %collective-permute-start.3 = (bf16[32,3072]{1,0:T(8,128)(2,1)S(1)}, bf16[32,3072]{1,0:T(8,128)(2,1)S(1)}, u32[]{:S(2)}, u32[]{:S(2)}) collective-permute-start(bf16[32,3072]{1,0:T(8,128)(2,1)S(1)} %convolution_convert_fusion.3), channel_id=1, source_target_pairs={{1,0},{0,1},{3,2},{2,3},{5,4},{4,5},{7,6},{6,7},{9,8},{8,9},{11,10... | collective-permute-start | bytes 589832 | tf_op jit(solution)/shard_map/ppermute | solution.py:22
  22.0 29.8 %collective-permute-start.5 = (bf16[32,3072]{1,0:T(8,128)(2,1)S(1)}, bf16[32,3072]{1,0:T(8,128)(2,1)S(1)}, u32[]{:S(2)}, u32[]{:S(2)}) collective-permute-start(bf16[32,3072]{1,0:T(8,128)(2,1)S(1)} %collective-permute-done.4), channel_id=1, source_target_pairs={{1,0},{0,1},{3,2},{2,3},{5,4},{4,5},{7,6},{6,7},{9,8},{8,9},{11,10... | collective-permute-start | bytes 589832 | tf_op jit(solution)/shard_map/ppermute | solution.py:22
  23.5 29.8 %collective-permute-start.7 = (bf16[32,3072]{1,0:T(8,128)(2,1)S(1)}, bf16[32,3072]{1,0:T(8,128)(2,1)S(1)}, u32[]{:S(2)}, u32[]{:S(2)}) collective-permute-start(bf16[32,3072]{1,0:T(8,128)(2,1)S(1)} %collective-permute-done.6), channel_id=1, source_target_pairs={{1,0},{0,1},{3,2},{2,3},{5,4},{4,5},{7,6},{6,7},{9,8},{8,9},{11,10... | collective-permute-start | bytes 589832 | tf_op jit(solution)/shard_map/ppermute | solution.py:22
  24.0 13.1 %collective-permute-start.2 = (bf16[32,3072]{1,0:T(8,128)(2,1)S(1)}, bf16[32,3072]{1,0:T(8,128)(2,1)S(1)}, u32[]{:S(2)}, u32[]{:S(2)}) collective-permute-start(bf16[32,3072]{1,0:T(8,128)(2,1)S(1)} %collective-permute-done.1), channel_id=1, source_target_pairs={{1,0},{0,1},{3,2},{2,3},{5,4},{4,5},{7,6},{6,7},{9,8},{8,9},{11,10... | collective-permute-start | bytes 589832 | tf_op jit(solution)/shard_map/ppermute | solution.py:22
  37.2 16.7 %collective-permute-start.13 = (bf16[32,3072]{1,0:T(8,128)(2,1)S(1)}, bf16[32,3072]{1,0:T(8,128)(2,1)S(1)}, u32[]{:S(2)}, u32[]{:S(2)}) collective-permute-start(bf16[32,3072]{1,0:T(8,128)(2,1)S(1)} %multiply_convert_fusion.1), channel_id=1, source_target_pairs={{24,0},{0,8},{8,16},{16,24},{25,1},{1,9},{9,17},{17,25},{26,2},{2,... | collective-permute-start | bytes 589832 | tf_op jit(solution)/shard_map/ppermute | solution.py:22
  39.7 15.7 %collective-permute-start.15 = (bf16[32,3072]{1,0:T(8,128)(2,1)S(1)}, bf16[32,3072]{1,0:T(8,128)(2,1)S(1)}, u32[]{:S(2)}, u32[]{:S(2)}) collective-permute-start(bf16[32,3072]{1,0:T(8,128)(2,1)S(1)} %multiply_convert_fusion.1), channel_id=1, source_target_pairs={{16,0},{24,8},{0,16},{8,24},{17,1},{25,9},{1,17},{9,25},{18,2},{26... | collective-permute-start | bytes 589832 | tf_op jit(solution)/shard_map/ppermute | solution.py:22
  43.1 13.1 %collective-permute-start.17 = (bf16[32,3072]{1,0:T(8,128)(2,1)S(1)}, bf16[32,3072]{1,0:T(8,128)(2,1)}, u32[]{:S(2)}, u32[]{:S(2)}) collective-permute-start(bf16[32,3072]{1,0:T(8,128)(2,1)S(1)} %multiply_convert_fusion.1), channel_id=1, source_target_pairs={{8,0},{16,8},{24,16},{0,24},{9,1},{17,9},{25,17},{1,25},{10,2},{18... | collective-permute-start | bytes 589832 | tf_op jit(solution)/shard_map/ppermute | solution.py:22
  51.8 21.9 %collective-permute-start.9 = (bf16[32,3072]{1,0:T(8,128)(2,1)S(1)}, bf16[32,3072]{1,0:T(8,128)(2,1)}, u32[]{:S(2)}, u32[]{:S(2)}) collective-permute-start(bf16[32,3072]{1,0:T(8,128)(2,1)S(1)} %collective-permute-done.8), channel_id=1, source_target_pairs={{1,0},{0,1},{3,2},{2,3},{5,4},{4,5},{7,6},{6,7},{9,8},{8,9},{11,10... | collective-permute-start | bytes 589832 | tf_op jit(solution)/shard_map/ppermute | solution.py:22
  53.4 20.3 %collective-permute-start.12 = (bf16[32,3072]{1,0:T(8,128)(2,1)S(1)}, bf16[32,3072]{1,0:T(8,128)(2,1)}, u32[]{:S(2)}, u32[]{:S(2)}) collective-permute-start(bf16[32,3072]{1,0:T(8,128)(2,1)S(1)} %multiply_convert_fusion.1), channel_id=1, source_target_pairs={{1,0},{0,1},{3,2},{2,3},{5,4},{4,5},{7,6},{6,7},{9,8},{8,9},{11,10... | collective-permute-start | bytes 589832 | tf_op jit(solution)/shard_map/ppermute | solution.py:22
  53.9 19.8 %collective-permute-start.14 = (bf16[32,3072]{1,0:T(8,128)(2,1)S(1)}, bf16[32,3072]{1,0:T(8,128)(2,1)}, u32[]{:S(2)}, u32[]{:S(2)}) collective-permute-start(bf16[32,3072]{1,0:T(8,128)(2,1)S(1)} %collective-permute-done.13), channel_id=1, source_target_pairs={{1,0},{0,1},{3,2},{2,3},{5,4},{4,5},{7,6},{6,7},{9,8},{8,9},{11,10... | collective-permute-start | bytes 589832 | tf_op jit(solution)/shard_map/ppermute | solution.py:22
  55.4 18.3 %collective-permute-start.16 = (bf16[32,3072]{1,0:T(8,128)(2,1)S(1)}, bf16[32,3072]{1,0:T(8,128)(2,1)}, u32[]{:S(2)}, u32[]{:S(2)}) collective-permute-start(bf16[32,3072]{1,0:T(8,128)(2,1)S(1)} %collective-permute-done.15), channel_id=1, source_target_pairs={{1,0},{0,1},{3,2},{2,3},{5,4},{4,5},{7,6},{6,7},{9,8},{8,9},{11,10... | collective-permute-start | bytes 589832 | tf_op jit(solution)/shard_map/ppermute | solution.py:22
  56.2 17.5 %collective-permute-start.18 = (bf16[32,3072]{1,0:T(8,128)(2,1)}, bf16[32,3072]{1,0:T(8,128)(2,1)}, u32[]{:S(2)}, u32[]{:S(2)}) collective-permute-start(bf16[32,3072]{1,0:T(8,128)(2,1)} %collective-permute-done.17), channel_id=1, source_target_pairs={{1,0},{0,1},{3,2},{2,3},{5,4},{4,5},{7,6},{6,7},{9,8},{8,9},{11,10... | collective-permute-start | bytes 589832 | tf_op jit(solution)/shard_map/ppermute | solution.py:22
  117.4 11.5 %copy-start.1 = (bf16[1,128,3072]{2,1,0:T(8,128)(2,1)S(1)}, bf16[1,128,3072]{2,1,0:T(8,128)(2,1)}, u32[]{:S(2)}) copy-start(bf16[1,128,3072]{2,1,0:T(8,128)(2,1)} %param.13) | copy-start | bytes 2359300
  117.4 7.7 %collective-permute-start.20 = (bf16[32,3072]{1,0:T(8,128)(2,1)S(1)}, bf16[32,3072]{1,0:T(8,128)(2,1)S(1)}, u32[]{:S(2)}, u32[]{:S(2)}) collective-permute-start(bf16[32,3072]{1,0:T(8,128)(2,1)S(1)} %slice.15), channel_id=1, source_target_pairs={{1,0},{0,1},{3,2},{2,3},{5,4},{4,5},{7,6},{6,7},{9,8},{8,9},{11,10... | collective-permute-start | bytes 589832 | tf_op jit(solution)/shard_map/ppermute | solution.py:22
  119.0 8.2 %collective-permute-start.19 = (bf16[32,3072]{1,0:T(8,128)(2,1)S(1)}, bf16[32,3072]{1,0:T(8,128)(2,1)S(1)}, u32[]{:S(2)}, u32[]{:S(2)}) collective-permute-start(bf16[32,3072]{1,0:T(8,128)(2,1)S(1)} %slice.13), channel_id=1, source_target_pairs={{1,0},{0,1},{3,2},{2,3},{5,4},{4,5},{7,6},{6,7},{9,8},{8,9},{11,10... | collective-permute-start | bytes 589832 | tf_op jit(solution)/shard_map/ppermute | solution.py:22
  (4 other events, 31.9 us)

commit v3 on v2

--- a/solution.py
+++ b/solution.py
@@ -47,20 +47,16 @@
     return lax.all_gather(rows, "et", axis=0, tiled=True)
 
 
-def scatter_et(partial):
+def sent_part(partial):
     if lax.axis_size("et") == 2:
-        other = passed_along(partial[CAP:], "et", 1)
-        return partial[:CAP].astype(jnp.float32) + other.astype(jnp.float32)
+        return passed_along(partial[CAP:], "et", 1).astype(jnp.float32)
     return lax.psum_scatter(partial, "et", scatter_dimension=0, tiled=True).astype(jnp.float32)
 
 
-def gather_replicas(rows):
+def with_own(partial, sent):
     if lax.axis_size("et") == 2:
-        blocks = [rows] + [passed_along(rows, "dp", d) for d in range(1, lax.axis_size("dp"))]
-        pairs = [piece for block in blocks for piece in (block, passed_along(block, "et", 1))]
-        return pairs, 0
-    own = lax.axis_index("dp") * lax.axis_size("et") * rows.shape[0]
-    return [lax.all_gather(rows, ("dp", "et"), axis=0, tiled=True)], own
+        return partial[:CAP].astype(jnp.float32) + sent
+    return sent
 
 
 def gates(pre_gate, pre_up, grad_hidden):
@@ -72,27 +68,21 @@
     return hidden, grad_gate, grad_up
 
 
-def back_kernel(
-    own_rows,
-    back_ref,
-    grad_ref,
-    back_cols,
-    grad_cols,
-    gate_ref,
-    up_ref,
-    down_ref,
-    gate_out,
-    up_out,
-    down_out,
-    rows_out,
-    total,
-    back_cols_t,
-):
+def back_kernel(own_rows, n_pieces, *refs):
+    pieces, refs = refs[:n_pieces], refs[n_pieces:]
+    gate_ref, up_ref, down_ref, gate_out, up_out, down_out, rows_out = refs[:7]
+    back_ref, grad_ref, back_cols_t, grad_cols, total = refs[7:]
     step = pl.program_id(0)
+    share = grad_cols.shape[1]
 
     @pl.when(step == 0)
     def _():
-        back_cols_t[...] = back_cols[...].T
+        for k, piece in enumerate(pieces):
+            back_ref[k * CAP : (k + 1) * CAP] = piece[:CAP]
+            grad_ref[k * CAP : (k + 1) * CAP] = piece[CAP:]
+        columns = pl.ds(pl.multiple_of(lax.axis_index("dp") * share, 128), share)
+        back_cols_t[...] = back_ref[:, columns].T
+        grad_cols[...] = grad_ref[:, columns]
 
     pre_gate = mul(back_ref[...], gate_ref[...])
     pre_up = mul(back_ref[...], up_ref[...])
@@ -117,9 +107,9 @@
         rows_out[...] = total[...].astype(jnp.bfloat16)
 
 
-def backward(back_all, grad_all, back_cols, grad_cols, gate_w, up_w, down_w, tile):
-    rows, depth = back_all.shape
-    share = back_cols.shape[1]
+def backward(pieces, gate_w, up_w, down_w, tile):
+    rows, depth = len(pieces) * CAP, gate_w.shape[0]
+    share = depth // lax.axis_size("dp")
     units = gate_w.shape[1]
     own_rows = rows // lax.axis_size("dp")
     whole = lambda i: (0, 0)
@@ -128,13 +118,10 @@
     down = lambda i: (i, 0)
     flops = 2 * units * (3 * rows * depth + 2 * own_rows * depth + 3 * rows * share)
     return pl.pallas_call(
-        functools.partial(back_kernel, own_rows),
+        functools.partial(back_kernel, own_rows, len(pieces)),
         grid=(units // tile,),
-        in_specs=[
-            once((rows, depth)),
-            once((rows, depth)),
-            once((rows, share)),
-            once((rows, share)),
+        in_specs=[once((2 * CAP, depth)) for _ in pieces]
+        + [
             pl.BlockSpec((depth, tile), across),
             pl.BlockSpec((depth, tile), across),
             pl.BlockSpec((tile, depth), down),
@@ -152,8 +139,11 @@
             jax.ShapeDtypeStruct((own_rows, depth), jnp.bfloat16),
         ],
         scratch_shapes=[
+            pltpu.VMEM((rows, depth), jnp.bfloat16),
+            pltpu.VMEM((rows, depth), jnp.bfloat16),
+            pltpu.VMEM((share, rows), jnp.bfloat16),
+            pltpu.VMEM((rows, share), jnp.bfloat16),
             pltpu.VMEM((own_rows, depth), jnp.float32),
-            pltpu.VMEM((share, rows), jnp.bfloat16),
         ],
         compiler_params=pltpu.CompilerParams(vmem_limit_bytes=48 * 2**20),
         cost_estimate=pl.CostEstimate(
@@ -161,10 +151,14 @@
             bytes_accessed=6 * units * (depth + share) + 8 * rows * depth,
             transcendentals=rows * units,
         ),
-    )(back_all, grad_all, back_cols, grad_cols, gate_w, up_w, down_w)
-
-
-def backward_plain(back_all, grad_all, back_cols, grad_cols, gate_w, up_w, down_w, start):
+    )(*pieces, gate_w, up_w, down_w)
+
+
+def backward_plain(back_all, grad_all, gate_w, up_w, down_w, start):
+    share = gate_w.shape[0] // lax.axis_size("dp")
+    first = lax.axis_index("dp") * share
+    back_cols = lax.dynamic_slice_in_dim(back_all, first, share, 1)
+    grad_cols = lax.dynamic_slice_in_dim(grad_all, first, share, 1)
     pre_gate, pre_up = mul(back_all, gate_w), mul(back_all, up_w)
     hidden, grad_gate, grad_up = gates(pre_gate, pre_up, mul(grad_all, down_w, NT))
     own_rows = back_all.shape[0] // lax.axis_size("dp")
@@ -192,40 +186,50 @@
 ):
     gate_w, up_w, down_w = (w_gate[0], w_up[0], w_down[0])
     fwd_ids, back_ids = fwd_slot[0], back_slot[0]
+    fwd_ids_there = passed_along(fwd_slot, "section", -1)[0]
     back_ids_there = passed_along(back_slot, "section", 1)[0]
-    fwd_ids_there = passed_along(fwd_slot, "section", -1)[0]
+    arrived = passed_along(pack_rows(handoff[0], fwd_ids_there), "section", 1)
+    returned = passed_along(pack_rows(grad_handoff[0], back_ids_there), "section", -1)
     stash_packed = pack_rows(stashed[0], back_ids)
-    back_pieces, own = gather_replicas(stash_packed)
-    returned = passed_along(pack_rows(grad_handoff[0], back_ids_there), "section", -1)
     weights = pack_values(back_weight[0], back_ids)
     grad_packed = (weights[:, None] * returned.astype(jnp.float32)).astype(jnp.bfloat16)
-    grad_pieces = gather_replicas(grad_packed)[0]
-
-    arrived = passed_along(pack_rows(handoff[0], fwd_ids_there), "section", 1)
-    fwd_rows = gather_et(arrived)
+    n_dp, n_et = lax.axis_size("dp"), lax.axis_size("et")
+
+    if n_et == 2:
+        block = jnp.concatenate([stash_packed, grad_packed], axis=0)
+        arrived, block = lax.optimization_barrier((arrived, block))
+        blocks = [passed_along(block, "dp", d) for d in range(1, n_dp)]
+        fwd_rows, block = lax.optimization_barrier((gather_et(arrived), block))
+        blocks = [block] + blocks
+        pieces = [x for one in blocks for x in (one, passed_along(one, "et", 1))]
+    else:
+        fwd_rows = gather_et(arrived)
+        pieces = [
+            lax.all_gather(x, ("dp", "et"), axis=0, tiled=True) for x in (stash_packed, grad_packed)
+        ]
+
     pre_gate = mul(fwd_rows, gate_w)
     pre_up = mul(fwd_rows, up_w)
     hidden = (pre_gate * jax.nn.sigmoid(pre_gate) * pre_up).astype(jnp.bfloat16)
     fwd_partial = mul(hidden, down_w).astype(jnp.bfloat16)
-    fwd_partial, back_pieces, grad_pieces = lax.optimization_barrier(
-        (fwd_partial, back_pieces, grad_pieces)
-    )
-    own_sum = scatter_et(fwd_partial)
+    sent, pieces = lax.optimization_barrier((sent_part(fwd_partial), pieces))
+    own_sum = with_own(fwd_partial, sent)
     forward_out = (fwd_weight[0][:, None] * unpack_rows(own_sum, fwd_ids)).astype(jnp.bfloat16)
 
-    back_all = jnp.concatenate(back_pieces, axis=0)
-    grad_all = jnp.concatenate(grad_pieces, axis=0)
-    share = gate_w.shape[0] // lax.axis_size("dp")
-    first = lax.axis_index("dp") * share
-    back_cols = lax.dynamic_slice_in_dim(back_all, first, share, 1)
-    grad_cols = lax.dynamic_slice_in_dim(grad_all, first, share, 1)
-    operands = (back_all, grad_all, back_cols, grad_cols, gate_w, up_w, down_w)
     tiles = [t for t in (384, 256, 128) if gate_w.shape[1] % t == 0]
-    if tiles and lax.axis_size("et") == 2 and back_all.shape[0] <= 512:
-        gate_sum, up_sum, down_sum, partial = backward(*operands, tiles[0])
+    aligned = gate_w.shape[0] % (128 * n_dp) == 0
+    if n_et == 2 and tiles and aligned and n_dp <= 8:
+        grads = backward(pieces, gate_w, up_w, down_w, tiles[0])
     else:
-        gate_sum, up_sum, down_sum, partial = backward_plain(*operands, own)
-    grad_rows = unpack_rows(scatter_et(partial), back_ids).astype(jnp.bfloat16)
+        own = 0
+        if n_et == 2:
+            pieces = [jnp.concatenate([x[k : k + CAP] for x in pieces]) for k in (0, CAP)]
+        else:
+            own = lax.axis_index("dp") * n_et * CAP
+        grads = backward_plain(*pieces, gate_w, up_w, down_w, own)
+    gate_sum, up_sum, down_sum, partial = grads
+    own_grad = with_own(partial, sent_part(partial))
+    grad_rows = unpack_rows(own_grad, back_ids).astype(jnp.bfloat16)
     return (
         forward_out[None],
         grad_rows[None],

time: 131 us -> 126 us (0.962); the launches traced: 129 us -> 126 us
  starting transfers between devices: 28.4 us -> 14.4 us
  waiting for transfers between devices: 24.1 us -> 34.6 us
  local copies, waits for them, and re-layouts: 5.97 us -> 2.72 us
  matrix products: 30.8 us -> 33.7 us
    ppermute x21 -> x14, starting transfers between devices: 28.4 us -> 14.4 us  [passed_along(): lax.ppermute(block, axis, [((i - distance) % n, i) for i in range(n)])]
    ppermute x21 -> x14, waiting for transfers between devices: 24.1 us -> 34.6 us  [passed_along(): lax.ppermute(block, axis, [((i - distance) % n, i) for i in range(n)])]
    unnamed x29 -> x16, local copies, waits for them, and re-layouts: 4.79 us -> 1.77 us
    dot_general x5, matrix products: 27.3 us -> 30.3 us  [mul(): return lax.dot_general(a, b, dims, preferred_element_type=jnp.float32)]
  transfers between devices with their start and end apart: 21 -> 14, of which waited for: 5 -> 6; matrix products, arithmetic and copies ran while one was open for 23% -> 27% of each run, Pallas kernels for 0% -> 0%
where the time goes in v3:
time: 126 us
  Pallas kernels  38.9 us (31%)
  waiting for transfers between devices  34.6 us (27%)
  matrix products  33.7 us (27%)
  starting transfers between devices  14.4 us (11%)
  local copies, waits for them, and re-layouts  2.72 us (2%)
    pallas_call x1, Pallas kernels, backward(): pl.pallas_call(functools.partial(back_kernel, own_rows, len(pieces)), gri...  38.9 us
    ppermute x14, waiting for transfers between devices, passed_along(): lax.ppermute(block, axis, [((i - distance) % n, i) for i in range(n)])  34.6 us
    dot_general x5, matrix products, mul(): return lax.dot_general(a, b, dims, preferred_element_type=jnp.float32)  30.3 us
    ppermute x14, starting transfers between devices, passed_along(): lax.ppermute(block, axis, [((i - distance) % n, i) for i in range(n)])  14.4 us
    dot_general x2, matrix products, unpack_rows(): jnp.dot(picker, packed, precision=lax.Precision.HIGHEST, preferred_elemen...  3.42 us
  transfers between devices with their start and end apart: 14, of which 6 were waited for; matrix products, arithmetic and copies ran while one was open for 27% of the time, Pallas kernels for 0%

profile of v3, /device:TPU:0, one launch (start us, length us, event | category | flops | bytes accessed | tf_op | source)
XLA Modules:
  0.0 126.1 jit_solution(15667740175439766688)
XLA Ops:
  0.6 2.4 %collective-permute-start = (s32[1,128]{1,0:T(1,128)}, s32[1,128]{1,0:T(1,128)S(1)}, u32[]{:S(2)}, u32[]{:S(2)}) collective-permute-start(s32[1,128]{1,0:T(1,128)} %param.11), channel_id=1, source_target_pairs={{2,0},{4,2},{6,4},{0,6},{3,1},{5,3},{7,5},{1,7},{10,8},{12,10},{14... | collective-permute-start | bytes 1544 | tf_op jit(solution)/shard_map/ppermute | solution.py:22
  3.1 0.9 convolution_convert_fusion.3
  4.0 0.8 select_reduce_fusion
  4.8 1.4 %collective-permute-done.2 = s32[1,128]{1,0:T(1,128)S(1)} collective-permute-done((s32[1,128]{1,0:T(1,128)}, s32[1,128]{1,0:T(1,128)S(1)}, u32[]{:S(2)}, u32[]{:S(2)}) %collective-permute-start.2) | collective-permute-done | bytes 544 | tf_op jit(solution)/shard_map/ppermute | solution.py:22
  6.2 1.4 %convolution_convert_fusion.2 = bf16[32,3072]{1,0:T(8,128)(2,1)S(1)} fusion(bf16[1,128,3072]{2,1,0:T(8,128)(2,1)} %param.16, s32[128]{0:T(128)S(1)} %bitcast.41), kind=kOutput, calls=%fused_computation.8 | convolution fusion | flops 25268224 | bytes 983552 | tf_op jit(solution)/shard_map/dot_general | solution.py:17
  8.0 1.4 %convolution_convert_fusion.4 = bf16[32,3072]{1,0:T(8,128)(2,1)S(1)} fusion(bf16[1,128,3072]{2,1,0:T(8,128)(2,1)} %param.10, s32[128]{0:T(128)S(1)} %bitcast.40), kind=kOutput, calls=%fused_computation.10 | convolution fusion | flops 25268224 | bytes 983552 | tf_op jit(solution)/shard_map/dot_general | solution.py:17
  9.5 2.2 %collective-permute-done.3 = bf16[32,3072]{1,0:T(8,128)(2,1)S(1)} collective-permute-done((bf16[32,3072]{1,0:T(8,128)(2,1)S(1)}, bf16[32,3072]{1,0:T(8,128)(2,1)S(1)}, u32[]{:S(2)}, u32[]{:S(2)}) %collective-permute-start.3) | collective-permute-done | bytes 196640 | tf_op jit(solution)/shard_map/ppermute | solution.py:22
  11.9 2.6 %collective-permute-done.1 = bf16[32,3072]{1,0:T(8,128)(2,1)S(1)} collective-permute-done((bf16[32,3072]{1,0:T(8,128)(2,1)S(1)}, bf16[32,3072]{1,0:T(8,128)(2,1)S(1)}, u32[]{:S(2)}, u32[]{:S(2)}) %collective-permute-start.1) | collective-permute-done | bytes 196640 | tf_op jit(solution)/shard_map/ppermute | solution.py:22
  14.5 1.5 %collective-permute-start.4 = (bf16[32,3072]{1,0:T(8,128)(2,1)S(1)}, bf16[32,3072]{1,0:T(8,128)(2,1)S(1)}, u32[]{:S(2)}, u32[]{:S(2)}) collective-permute-start(bf16[32,3072]{1,0:T(8,128)(2,1)S(1)} %collective-permute-done.1), channel_id=1, source_target_pairs={{1,0},{0,1},{3,2},{2,3},{5,4},{4,5},{7,6},{6,7},{9,8},{8,9},{11,10... | collective-permute-start | bytes 589832 | tf_op jit(solution)/shard_map/ppermute | solution.py:22
  16.0 3.6 %collective-permute-start.11 = (bf16[64,3072]{1,0:T(8,128)(2,1)S(1)}, bf16[64,3072]{1,0:T(8,128)(2,1)S(1)}, u32[]{:S(2)}, u32[]{:S(2)}) collective-permute-start(bf16[64,3072]{1,0:T(8,128)(2,1)S(1)} %pad_maximum_fusion.refs_0_), channel_id=1, source_target_pairs={{8,0},{16,8},{24,16},{0,24},{9,1},{17,9},{25,17},{1,25},{10,2},{18... | collective-permute-start | bytes 1179656 | tf_op jit(solution)/shard_map/ppermute | solution.py:22
  19.6 1.0 collective-permute-start.7
  20.7 1.1 collective-permute-start.6
  21.8 9.5 %fusion.23 = f32[64,2688]{1,0:T(8,128)} fusion(bf16[64,3072]{1,0:T(8,128)(2,1)S(1)} %pad_maximum_fusion.1, bf16[1,3072,2688]{2,1,0:T(8,128)(2,1)} %param.17), kind=kOutput, calls=%fused_computation.38 | convolution fusion | flops 1056964608 | bytes 17596416 | tf_op jit(solution)/shard_map/dot_general | solution.py:17
  31.3 1.0 collective-permute-start.12
  32.2 19.7 %collective-permute-done.9.refs_4_ = bf16[64,3072]{1,0:T(8,128)(2,1)S(1)} collective-permute-done((bf16[64,3072]{1,0:T(8,128)(2,1)S(1)}, bf16[64,3072]{1,0:T(8,128)(2,1)S(1)}, u32[]{:S(2)}, u32[]{:S(2)}) %collective-permute-start.9) | collective-permute-done | bytes 393248 | tf_op jit(solution)/shard_map/ppermute | solution.py:22
  52.4 1.5 %collective-permute-start.8 = (bf16[64,3072]{1,0:T(8,128)(2,1)S(1)}, bf16[64,3072]{1,0:T(8,128)(2,1)S(1)}, u32[]{:S(2)}, u32[]{:S(2)}) collective-permute-start(bf16[64,3072]{1,0:T(8,128)(2,1)S(1)} %collective-permute-done.7.refs_2_), channel_id=1, source_target_pairs={{1,0},{0,1},{3,2},{2,3},{5,4},{4,5},{7,6},{6,7},{9,8},{8,9},{11,10... | collective-permute-start | bytes 1179656 | tf_op jit(solution)/shard_map/ppermute | solution.py:22
  54.0 17.2 %convolution_convert_fusion.1 = bf16[64,3072]{1,0:T(8,128)(2,1)} fusion(bf16[64,3072]{1,0:T(8,128)(2,1)S(1)} %pad_maximum_fusion.1, f32[64,2688]{1,0:T(8,128)} %fusion.23, bf16[1,2688,3072]{2,1,0:T(8,128)(2,1)} %param.19, bf16[1,3072,2688]{2,1,0:T(8,128)(2,1)} %param.18), kind=kOutput, calls=%fused_computation.7 | convolution fusion | flops 2115158016 | bytes 34504704 | tf_op jit(solution)/shard_map/dot_general | solution.py:17
  71.2 0.9 slice.17
  72.7 5.2 %collective-permute-done.5 = bf16[32,3072]{1,0:T(8,128)(2,1)S(1)} collective-permute-done((bf16[32,3072]{1,0:T(8,128)(2,1)S(1)}, bf16[32,3072]{1,0:T(8,128)(2,1)S(1)}, u32[]{:S(2)}, u32[]{:S(2)}) %collective-permute-start.5) | collective-permute-done | bytes 196640 | tf_op jit(solution)/shard_map/ppermute | solution.py:22
  78.7 1.0 copy-done.3
  79.7 38.9 %shard_map.137 = (bf16[768,2688]{1,0:T(8,128)(2,1)}, bf16[768,2688]{1,0:T(8,128)(2,1)}, bf16[2688,768]{1,0:T(8,128)(2,1)}, bf16[64,3072]{1,0:T(8,128)(2,1)S(1)}) custom-call(bf16[64,3072]{1,0:T(8,128)(2,1)S(1)} %pad_maximum_fusion.refs_0_, bf16[64,3072]{1,0:T(8,128)(2,1)S(1)} %collective-permute-done.6.refs_1_, ...), custom_call_target="tpu_custom_call" | custom-call | flops 17968398336 | bytes 68222976 | tf_op jit(solution)/shard_map/pallas_call | solution.py:120
  119.2 1.7 %fusion.2 = bf16[1,128,3072]{2,1,0:T(8,128)(2,1)} fusion(f32[128]{0:T(128)S(1)} %bitcast.42, f32[32,3072]{1,0:T(8,128)S(1)} %convert_element_type.52, bf16[64,3072]{1,0:T(8,128)(2,1)S(1)} %copy-done.4, s32[128]{0:T(128)S(1)} %bitcast.43), kind=kOutput, calls=%fused_computation.5 | convolution fusion | flops 151982080 | bytes 1377280 | tf_op jit(solution)/shard_map/dot_general | solution.py:39
  120.9 3.4 %collective-permute-done.13 = bf16[32,3072]{1,0:T(8,128)(2,1)S(1)} collective-permute-done((bf16[32,3072]{1,0:T(8,128)(2,1)S(1)}, bf16[32,3072]{1,0:T(8,128)(2,1)S(1)}, u32[]{:S(2)}, u32[]{:S(2)}) %collective-permute-start.13) | collective-permute-done | bytes 196640 | tf_op jit(solution)/shard_map/ppermute | solution.py:22
  124.4 1.7 %fusion.1 = bf16[1,128,3072]{2,1,0:T(8,128)(2,1)} fusion(bf16[32,3072]{1,0:T(8,128)(2,1)S(1)} %collective-permute-done.13, bf16[64,3072]{1,0:T(8,128)(2,1)S(1)} %get-tuple-element.35, s32[128]{0:T(128)S(1)} %bitcast.39), kind=kOutput, calls=%fused_computation.4 | convolution fusion | flops 151687168 | bytes 1180160 | tf_op jit(solution)/shard_map/dot_general | solution.py:39
  (35 shorter events, 3.3 us)
Async XLA Ops:
  0.6 2.5 %copy-start = (bf16[1,128,3072]{2,1,0:T(8,128)(2,1)S(1)}, bf16[1,128,3072]{2,1,0:T(8,128)(2,1)}, u32[]{:S(2)}) copy-start(bf16[1,128,3072]{2,1,0:T(8,128)(2,1)} %param.13) | copy-start | bytes 2359300
  0.6 7.3 %collective-permute-start = (s32[1,128]{1,0:T(1,128)}, s32[1,128]{1,0:T(1,128)S(1)}, u32[]{:S(2)}, u32[]{:S(2)}) collective-permute-start(s32[1,128]{1,0:T(1,128)} %param.11), channel_id=1, source_target_pairs={{2,0},{4,2},{6,4},{0,6},{3,1},{5,3},{7,5},{1,7},{10,8},{12,10},{14... | collective-permute-start | bytes 1544 | tf_op jit(solution)/shard_map/ppermute | solution.py:22
  3.1 3.1 %collective-permute-start.2 = (s32[1,128]{1,0:T(1,128)}, s32[1,128]{1,0:T(1,128)S(1)}, u32[]{:S(2)}, u32[]{:S(2)}) collective-permute-start(s32[1,128]{1,0:T(1,128)} %param.14), channel_id=1, source_target_pairs={{6,0},{0,2},{2,4},{4,6},{7,1},{1,3},{3,5},{5,7},{14,8},{8,10},{10,... | collective-permute-start | bytes 1544 | tf_op jit(solution)/shard_map/ppermute | solution.py:22
  7.5 4.2 %collective-permute-start.3 = (bf16[32,3072]{1,0:T(8,128)(2,1)S(1)}, bf16[32,3072]{1,0:T(8,128)(2,1)S(1)}, u32[]{:S(2)}, u32[]{:S(2)}) collective-permute-start(bf16[32,3072]{1,0:T(8,128)(2,1)S(1)} %convolution_convert_fusion.2), channel_id=1, source_target_pairs={{2,0},{4,2},{6,4},{0,6},{3,1},{5,3},{7,5},{1,7},{10,8},{12,10},{14... | collective-permute-start | bytes 589832 | tf_op jit(solution)/shard_map/ppermute | solution.py:22
  9.3 5.1 %collective-permute-start.1 = (bf16[32,3072]{1,0:T(8,128)(2,1)S(1)}, bf16[32,3072]{1,0:T(8,128)(2,1)S(1)}, u32[]{:S(2)}, u32[]{:S(2)}) collective-permute-start(bf16[32,3072]{1,0:T(8,128)(2,1)S(1)} %convolution_convert_fusion.4), channel_id=1, source_target_pairs={{6,0},{0,2},{2,4},{4,6},{7,1},{1,3},{3,5},{5,7},{14,8},{8,10},{10,... | collective-permute-start | bytes 589832 | tf_op jit(solution)/shard_map/ppermute | solution.py:22
  14.5 6.1 %collective-permute-start.4 = (bf16[32,3072]{1,0:T(8,128)(2,1)S(1)}, bf16[32,3072]{1,0:T(8,128)(2,1)S(1)}, u32[]{:S(2)}, u32[]{:S(2)}) collective-permute-start(bf16[32,3072]{1,0:T(8,128)(2,1)S(1)} %collective-permute-done.1), channel_id=1, source_target_pairs={{1,0},{0,1},{3,2},{2,3},{5,4},{4,5},{7,6},{6,7},{9,8},{8,9},{11,10... | collective-permute-start | bytes 589832 | tf_op jit(solution)/shard_map/ppermute | solution.py:22
  16.0 15.3 %collective-permute-start.11 = (bf16[64,3072]{1,0:T(8,128)(2,1)S(1)}, bf16[64,3072]{1,0:T(8,128)(2,1)S(1)}, u32[]{:S(2)}, u32[]{:S(2)}) collective-permute-start(bf16[64,3072]{1,0:T(8,128)(2,1)S(1)} %pad_maximum_fusion.refs_0_), channel_id=1, source_target_pairs={{8,0},{16,8},{24,16},{0,24},{9,1},{17,9},{25,17},{1,25},{10,2},{18... | collective-permute-start | bytes 1179656 | tf_op jit(solution)/shard_map/ppermute | solution.py:22
  19.6 32.3 %collective-permute-start.9 = (bf16[64,3072]{1,0:T(8,128)(2,1)S(1)}, bf16[64,3072]{1,0:T(8,128)(2,1)S(1)}, u32[]{:S(2)}, u32[]{:S(2)}) collective-permute-start(bf16[64,3072]{1,0:T(8,128)(2,1)S(1)} %pad_maximum_fusion.refs_0_), channel_id=1, source_target_pairs={{16,0},{24,8},{0,16},{8,24},{17,1},{25,9},{1,17},{9,25},{18,2},{26... | collective-permute-start | bytes 1179656 | tf_op jit(solution)/shard_map/ppermute | solution.py:22
  19.6 32.8 %collective-permute-start.7 = (bf16[64,3072]{1,0:T(8,128)(2,1)S(1)}, bf16[64,3072]{1,0:T(8,128)(2,1)S(1)}, u32[]{:S(2)}, u32[]{:S(2)}) collective-permute-start(bf16[64,3072]{1,0:T(8,128)(2,1)S(1)} %pad_maximum_fusion.refs_0_), channel_id=1, source_target_pairs={{24,0},{0,8},{8,16},{16,24},{25,1},{1,9},{9,17},{17,25},{26,2},{2,... | collective-permute-start | bytes 1179656 | tf_op jit(solution)/shard_map/ppermute | solution.py:22
  20.7 57.2 %collective-permute-start.6 = (bf16[64,3072]{1,0:T(8,128)(2,1)S(1)}, bf16[64,3072]{1,0:T(8,128)(2,1)S(1)}, u32[]{:S(2)}, u32[]{:S(2)}) collective-permute-start(bf16[64,3072]{1,0:T(8,128)(2,1)S(1)} %pad_maximum_fusion.refs_0_), channel_id=1, source_target_pairs={{1,0},{0,1},{3,2},{2,3},{5,4},{4,5},{7,6},{6,7},{9,8},{8,9},{11,10... | collective-permute-start | bytes 1179656 | tf_op jit(solution)/shard_map/ppermute | solution.py:22
  31.3 46.6 %collective-permute-start.12 = (bf16[64,3072]{1,0:T(8,128)(2,1)S(1)}, bf16[64,3072]{1,0:T(8,128)(2,1)S(1)}, u32[]{:S(2)}, u32[]{:S(2)}) collective-permute-start(bf16[64,3072]{1,0:T(8,128)(2,1)S(1)} %collective-permute-done.11.refs_6_), channel_id=1, source_target_pairs={{1,0},{0,1},{3,2},{2,3},{5,4},{4,5},{7,6},{6,7},{9,8},{8,9},{11,10... | collective-permute-start | bytes 1179656 | tf_op jit(solution)/shard_map/ppermute | solution.py:22
  51.9 26.0 %collective-permute-start.10 = (bf16[64,3072]{1,0:T(8,128)(2,1)S(1)}, bf16[64,3072]{1,0:T(8,128)(2,1)S(1)}, u32[]{:S(2)}, u32[]{:S(2)}) collective-permute-start(bf16[64,3072]{1,0:T(8,128)(2,1)S(1)} %collective-permute-done.9.refs_4_), channel_id=1, source_target_pairs={{1,0},{0,1},{3,2},{2,3},{5,4},{4,5},{7,6},{6,7},{9,8},{8,9},{11,10... | collective-permute-start | bytes 1179656 | tf_op jit(solution)/shard_map/ppermute | solution.py:22
  52.4 25.5 %collective-permute-start.8 = (bf16[64,3072]{1,0:T(8,128)(2,1)S(1)}, bf16[64,3072]{1,0:T(8,128)(2,1)S(1)}, u32[]{:S(2)}, u32[]{:S(2)}) collective-permute-start(bf16[64,3072]{1,0:T(8,128)(2,1)S(1)} %collective-permute-done.7.refs_2_), channel_id=1, source_target_pairs={{1,0},{0,1},{3,2},{2,3},{5,4},{4,5},{7,6},{6,7},{9,8},{8,9},{11,10... | collective-permute-start | bytes 1179656 | tf_op jit(solution)/shard_map/ppermute | solution.py:22
  72.1 5.7 %collective-permute-start.5 = (bf16[32,3072]{1,0:T(8,128)(2,1)S(1)}, bf16[32,3072]{1,0:T(8,128)(2,1)S(1)}, u32[]{:S(2)}, u32[]{:S(2)}) collective-permute-start(bf16[32,3072]{1,0:T(8,128)(2,1)S(1)} %slice.17), channel_id=1, source_target_pairs={{1,0},{0,1},{3,2},{2,3},{5,4},{4,5},{7,6},{6,7},{9,8},{8,9},{11,10... | collective-permute-start | bytes 589832 | tf_op jit(solution)/shard_map/ppermute | solution.py:22
  77.9 0.7 copy-start.2
  78.7 1.0 copy-start.3
  79.7 39.5 %copy-start.4 = (bf16[64,3072]{1,0:T(8,128)(2,1)S(1)}, bf16[64,3072]{1,0:T(8,128)(2,1)}, u32[]{:S(2)}) copy-start(bf16[64,3072]{1,0:T(8,128)(2,1)} %convolution_convert_fusion.1) | copy-start | bytes 1179652
  79.7 39.5 %copy-start.6 = (f32[1,128]{1,0:T(1,128)S(1)}, f32[1,128]{1,0:T(1,128)}, u32[]{:S(2)}) copy-start(f32[1,128]{1,0:T(1,128)} %param.12) | copy-start | bytes 1540
  79.7 39.5 %copy-start.7 = (s32[1,128]{1,0:T(1,128)S(1)}, s32[1,128]{1,0:T(1,128)}, u32[]{:S(2)}) copy-start(s32[1,128]{1,0:T(1,128)} %param.11) | copy-start | bytes 1540
  79.7 44.7 %copy-start.5 = (s32[1,128]{1,0:T(1,128)S(1)}, s32[1,128]{1,0:T(1,128)}, u32[]{:S(2)}) copy-start(s32[1,128]{1,0:T(1,128)} %param.14) | copy-start | bytes 1540
  79.7 46.4 %copy-start.1 = (bf16[1,128,3072]{2,1,0:T(8,128)(2,1)S(1)}, bf16[1,128,3072]{2,1,0:T(8,128)(2,1)}, u32[]{:S(2)}) copy-start(bf16[1,128,3072]{2,1,0:T(8,128)(2,1)} %param.13) | copy-start | bytes 2359300
  118.6 5.7 %collective-permute-start.13 = (bf16[32,3072]{1,0:T(8,128)(2,1)S(1)}, bf16[32,3072]{1,0:T(8,128)(2,1)S(1)}, u32[]{:S(2)}, u32[]{:S(2)}) collective-permute-start(bf16[32,3072]{1,0:T(8,128)(2,1)S(1)} %slice.15), channel_id=1, source_target_pairs={{1,0},{0,1},{3,2},{2,3},{5,4},{4,5},{7,6},{6,7},{9,8},{8,9},{11,10... | collective-permute-start | bytes 589832 | tf_op jit(solution)/shard_map/ppermute | solution.py:22

commit v4 on v3

--- a/solution.py
+++ b/solution.py
@@ -200,8 +200,6 @@
         arrived, block = lax.optimization_barrier((arrived, block))
         blocks = [passed_along(block, "dp", d) for d in range(1, n_dp)]
         fwd_rows, block = lax.optimization_barrier((gather_et(arrived), block))
-        blocks = [block] + blocks
-        pieces = [x for one in blocks for x in (one, passed_along(one, "et", 1))]
     else:
         fwd_rows = gather_et(arrived)
         pieces = [
@@ -209,9 +207,16 @@
         ]
 
     pre_gate = mul(fwd_rows, gate_w)
+    if n_et == 2:
+        pre_gate, last = lax.optimization_barrier((pre_gate, blocks[-1]))
     pre_up = mul(fwd_rows, up_w)
     hidden = (pre_gate * jax.nn.sigmoid(pre_gate) * pre_up).astype(jnp.bfloat16)
     fwd_partial = mul(hidden, down_w).astype(jnp.bfloat16)
+    if n_et == 2:
+        swapped = passed_along(last, "et", 1)
+        fwd_partial, early, swapped = lax.optimization_barrier((fwd_partial, blocks[:-1], swapped))
+        pieces = [x for one in [block] + early for x in (one, passed_along(one, "et", 1))]
+        pieces += [last, swapped]
     sent, pieces = lax.optimization_barrier((sent_part(fwd_partial), pieces))
     own_sum = with_own(fwd_partial, sent)
     forward_out = (fwd_weight[0][:, None] * unpack_rows(own_sum, fwd_ids)).astype(jnp.bfloat16)

time: 126 us -> 135 us (1.071)
  the two profiles are of different devices: /device:TPU:0 before, /device:TPU:8 now
where the time goes in v4:
time: 135 us
  waiting for transfers between devices  46.8 us (35%)
  Pallas kernels  38.8 us (29%)
  matrix products  33 us (24%)
  starting transfers between devices  14.7 us (11%)
    ppermute x14, waiting for transfers between devices, passed_along(): lax.ppermute(block, axis, [((i - distance) % n, i) for i in range(n)])  46.8 us
    pallas_call x1, Pallas kernels, backward(): pl.pallas_call(functools.partial(back_kernel, own_rows, len(pieces)), gri...  38.8 us
    dot_general x5, matrix products, mul(): return lax.dot_general(a, b, dims, preferred_element_type=jnp.float32)  29.5 us
    ppermute x14, starting transfers between devices, passed_along(): lax.ppermute(block, axis, [((i - distance) % n, i) for i in range(n)])  14.7 us
    dot_general x2, matrix products, unpack_rows(): jnp.dot(picker, packed, precision=lax.Precision.HIGHEST, preferred_elemen...  3.42 us
  transfers between devices with their start and end apart: 14, of which 6 were waited for; matrix products, arithmetic and copies ran while one was open for 24% of the time, Pallas kernels for 0%

profile of v4, /device:TPU:8, one launch (start us, length us, event | category | flops | bytes accessed | tf_op | source)
XLA Modules:
  0.0 135.1 jit_solution(6442950367600714675)
XLA Ops:
  0.6 1.0 collective-permute-start
  1.8 0.9 convolution_convert_fusion.3
  2.7 0.8 select_reduce_fusion
  3.5 1.3 collective-permute-done.2
  4.7 1.4 %convolution_convert_fusion.2 = bf16[32,3072]{1,0:T(8,128)(2,1)S(1)} fusion(bf16[1,128,3072]{2,1,0:T(8,128)(2,1)} %param.16, s32[128]{0:T(128)S(1)} %bitcast.44), kind=kOutput, calls=%fused_computation.6 | convolution fusion | flops 25268224 | bytes 983552 | tf_op jit(solution)/shard_map/dot_general | solution.py:17
  6.5 1.4 %convolution_convert_fusion.4 = bf16[32,3072]{1,0:T(8,128)(2,1)S(1)} fusion(bf16[1,128,3072]{2,1,0:T(8,128)(2,1)} %param.10, s32[128]{0:T(128)S(1)} %bitcast.43), kind=kOutput, calls=%fused_computation.8 | convolution fusion | flops 25268224 | bytes 983552 | tf_op jit(solution)/shard_map/dot_general | solution.py:17
  8.1 2.2 %collective-permute-done.3 = bf16[32,3072]{1,0:T(8,128)(2,1)S(1)} collective-permute-done((bf16[32,3072]{1,0:T(8,128)(2,1)S(1)}, bf16[32,3072]{1,0:T(8,128)(2,1)S(1)}, u32[]{:S(2)}, u32[]{:S(2)}) %collective-permute-start.3) | collective-permute-done | bytes 196640 | tf_op jit(solution)/shard_map/ppermute | solution.py:22
  10.4 2.6 %collective-permute-done.1 = bf16[32,3072]{1,0:T(8,128)(2,1)S(1)} collective-permute-done((bf16[32,3072]{1,0:T(8,128)(2,1)S(1)}, bf16[32,3072]{1,0:T(8,128)(2,1)S(1)}, u32[]{:S(2)}, u32[]{:S(2)}) %collective-permute-start.1) | collective-permute-done | bytes 196640 | tf_op jit(solution)/shard_map/ppermute | solution.py:22
  13.0 1.5 %collective-permute-start.4 = (bf16[32,3072]{1,0:T(8,128)(2,1)S(1)}, bf16[32,3072]{1,0:T(8,128)(2,1)S(1)}, u32[]{:S(2)}, u32[]{:S(2)}) collective-permute-start(bf16[32,3072]{1,0:T(8,128)(2,1)S(1)} %collective-permute-done.1), channel_id=1, source_target_pairs={{1,0},{0,1},{3,2},{2,3},{5,4},{4,5},{7,6},{6,7},{9,8},{8,9},{11,10... | collective-permute-start | bytes 589832 | tf_op jit(solution)/shard_map/ppermute | solution.py:22
  14.6 2.6 %collective-permute-start.7 = (bf16[64,3072]{1,0:T(8,128)(2,1)S(1)}, bf16[64,3072]{1,0:T(8,128)(2,1)S(1)}, u32[]{:S(2)}, u32[]{:S(2)}) collective-permute-start(bf16[64,3072]{1,0:T(8,128)(2,1)S(1)} %pad_maximum_fusion.refs_0_), channel_id=1, source_target_pairs={{16,0},{24,8},{0,16},{8,24},{17,1},{25,9},{1,17},{9,25},{18,2},{26... | collective-permute-start | bytes 1179656 | tf_op jit(solution)/shard_map/ppermute | solution.py:22
  17.2 2.0 %collective-permute-start.5 = (bf16[64,3072]{1,0:T(8,128)(2,1)S(1)}, bf16[64,3072]{1,0:T(8,128)(2,1)S(1)}, u32[]{:S(2)}, u32[]{:S(2)}) collective-permute-start(bf16[64,3072]{1,0:T(8,128)(2,1)S(1)} %pad_maximum_fusion.refs_0_), channel_id=1, source_target_pairs={{8,0},{16,8},{24,16},{0,24},{9,1},{17,9},{25,17},{1,25},{10,2},{18... | collective-permute-start | bytes 1179656 | tf_op jit(solution)/shard_map/ppermute | solution.py:22
  19.2 1.1 collective-permute-start.10
  20.4 9.5 %fusion.26 = f32[64,2688]{1,0:T(8,128)} fusion(bf16[64,3072]{1,0:T(8,128)(2,1)S(1)} %pad_maximum_fusion.1, bf16[1,3072,2688]{2,1,0:T(8,128)(2,1)} %param.17), kind=kOutput, calls=%fused_computation.38 | convolution fusion | flops 1056964608 | bytes 17596416 | tf_op jit(solution)/shard_map/dot_general | solution.py:17
  29.8 19.6 %collective-permute-done.5.refs_6_ = bf16[64,3072]{1,0:T(8,128)(2,1)S(1)} collective-permute-done((bf16[64,3072]{1,0:T(8,128)(2,1)S(1)}, bf16[64,3072]{1,0:T(8,128)(2,1)S(1)}, u32[]{:S(2)}, u32[]{:S(2)}) %collective-permute-start.5) | collective-permute-done | bytes 393248 | tf_op jit(solution)/shard_map/ppermute | solution.py:22
  49.4 0.5 collective-permute-start.8
  49.9 16.5 %convolution_convert_fusion.1 = bf16[64,3072]{1,0:T(8,128)(2,1)S(1)} fusion(f32[64,2688]{1,0:T(8,128)} %fusion.26, bf16[1,2688,3072]{2,1,0:T(8,128)(2,1)} %param.19, bf16[64,3072]{1,0:T(8,128)(2,1)S(1)} %pad_maximum_fusion.1, bf16[1,3072,2688]{2,1,0:T(8,128)(2,1)} %param.18), kind=kOutput, calls=%fused_computation.5 | convolution fusion | flops 2115158016 | bytes 34504704 | tf_op jit(solution)/shard_map/dot_general | solution.py:17
  66.4 1.6 %collective-permute-start.11 = (bf16[64,3072]{1,0:T(8,128)(2,1)S(1)}, bf16[64,3072]{1,0:T(8,128)(2,1)S(1)}, u32[]{:S(2)}, u32[]{:S(2)}) collective-permute-start(bf16[64,3072]{1,0:T(8,128)(2,1)S(1)} %collective-permute-done.6.refs_2_), channel_id=1, source_target_pairs={{1,0},{0,1},{3,2},{2,3},{5,4},{4,5},{7,6},{6,7},{9,8},{8,9},{11,10... | collective-permute-start | bytes 1179656 | tf_op jit(solution)/shard_map/ppermute | solution.py:22
  68.5 1.6 %collective-permute-start.9 = (bf16[32,3072]{1,0:T(8,128)(2,1)S(1)}, bf16[32,3072]{1,0:T(8,128)(2,1)S(1)}, u32[]{:S(2)}, u32[]{:S(2)}) collective-permute-start(bf16[32,3072]{1,0:T(8,128)(2,1)S(1)} %slice.13), channel_id=1, source_target_pairs={{1,0},{0,1},{3,2},{2,3},{5,4},{4,5},{7,6},{6,7},{9,8},{8,9},{11,10... | collective-permute-start | bytes 589832 | tf_op jit(solution)/shard_map/ppermute | solution.py:22
  70.1 18.7 %collective-permute-done.9 = bf16[32,3072]{1,0:T(8,128)(2,1)S(1)} collective-permute-done((bf16[32,3072]{1,0:T(8,128)(2,1)S(1)}, bf16[32,3072]{1,0:T(8,128)(2,1)S(1)}, u32[]{:S(2)}, u32[]{:S(2)}) %collective-permute-start.9) | collective-permute-done | bytes 196640 | tf_op jit(solution)/shard_map/ppermute | solution.py:22
  88.9 38.8 %shard_map.137 = (bf16[768,2688]{1,0:T(8,128)(2,1)}, bf16[768,2688]{1,0:T(8,128)(2,1)}, bf16[2688,768]{1,0:T(8,128)(2,1)}, bf16[64,3072]{1,0:T(8,128)(2,1)S(1)}) custom-call(bf16[64,3072]{1,0:T(8,128)(2,1)S(1)} %pad_maximum_fusion.refs_0_, bf16[64,3072]{1,0:T(8,128)(2,1)S(1)} %collective-permute-done.10.refs_1_, ...), custom_call_target="tpu_custom_call" | custom-call | flops 17968398336 | bytes 68222976 | tf_op jit(solution)/shard_map/pallas_call | solution.py:120
  127.7 1.6 %collective-permute-start.13 = (bf16[32,3072]{1,0:T(8,128)(2,1)S(1)}, bf16[32,3072]{1,0:T(8,128)(2,1)S(1)}, u32[]{:S(2)}, u32[]{:S(2)}) collective-permute-start(bf16[32,3072]{1,0:T(8,128)(2,1)S(1)} %slice.15), channel_id=1, source_target_pairs={{1,0},{0,1},{3,2},{2,3},{5,4},{4,5},{7,6},{6,7},{9,8},{8,9},{11,10... | collective-permute-start | bytes 589832 | tf_op jit(solution)/shard_map/ppermute | solution.py:22
  129.3 1.7 %fusion.2 = bf16[1,128,3072]{2,1,0:T(8,128)(2,1)} fusion(f32[128]{0:T(128)S(1)} %bitcast.45, f32[32,3072]{1,0:T(8,128)S(1)} %convert_element_type.52, bf16[64,3072]{1,0:T(8,128)(2,1)S(1)} %convolution_convert_fusion.1, s32[128]{0:T(128)S(1)} %bitcast.46), kind=kOutput, calls=%fused_computation.4 | convolution fusion | flops 151982080 | bytes 1377280 | tf_op jit(solution)/shard_map/dot_general | solution.py:39
  131.0 2.4 %collective-permute-done.13 = bf16[32,3072]{1,0:T(8,128)(2,1)S(1)} collective-permute-done((bf16[32,3072]{1,0:T(8,128)(2,1)S(1)}, bf16[32,3072]{1,0:T(8,128)(2,1)S(1)}, u32[]{:S(2)}, u32[]{:S(2)}) %collective-permute-start.13) | collective-permute-done | bytes 196640 | tf_op jit(solution)/shard_map/ppermute | solution.py:22
  133.4 1.7 %fusion.1 = bf16[1,128,3072]{2,1,0:T(8,128)(2,1)} fusion(bf16[32,3072]{1,0:T(8,128)(2,1)S(1)} %collective-permute-done.13, bf16[64,3072]{1,0:T(8,128)(2,1)S(1)} %get-tuple-element.47, s32[128]{0:T(128)S(1)} %bitcast.42), kind=kOutput, calls=%fused_computation.3 | convolution fusion | flops 151687168 | bytes 1180160 | tf_op jit(solution)/shard_map/dot_general | solution.py:39
  (29 shorter events, 1.5 us)
Async XLA Ops:
  0.6 1.1 copy-start
  0.6 5.9 %collective-permute-start = (s32[1,128]{1,0:T(1,128)}, s32[1,128]{1,0:T(1,128)S(1)}, u32[]{:S(2)}, u32[]{:S(2)}) collective-permute-start(s32[1,128]{1,0:T(1,128)} %param.11), channel_id=1, source_target_pairs={{2,0},{4,2},{6,4},{0,6},{3,1},{5,3},{7,5},{1,7},{10,8},{12,10},{14... | collective-permute-start | bytes 1544 | tf_op jit(solution)/shard_map/ppermute | solution.py:22
  1.6 3.1 %collective-permute-start.2 = (s32[1,128]{1,0:T(1,128)}, s32[1,128]{1,0:T(1,128)S(1)}, u32[]{:S(2)}, u32[]{:S(2)}) collective-permute-start(s32[1,128]{1,0:T(1,128)} %param.14), channel_id=1, source_target_pairs={{6,0},{0,2},{2,4},{4,6},{7,1},{1,3},{3,5},{5,7},{14,8},{8,10},{10,... | collective-permute-start | bytes 1544 | tf_op jit(solution)/shard_map/ppermute | solution.py:22
  6.1 4.2 %collective-permute-start.3 = (bf16[32,3072]{1,0:T(8,128)(2,1)S(1)}, bf16[32,3072]{1,0:T(8,128)(2,1)S(1)}, u32[]{:S(2)}, u32[]{:S(2)}) collective-permute-start(bf16[32,3072]{1,0:T(8,128)(2,1)S(1)} %convolution_convert_fusion.2), channel_id=1, source_target_pairs={{2,0},{4,2},{6,4},{0,6},{3,1},{5,3},{7,5},{1,7},{10,8},{12,10},{14... | collective-permute-start | bytes 589832 | tf_op jit(solution)/shard_map/ppermute | solution.py:22
  7.9 5.1 %collective-permute-start.1 = (bf16[32,3072]{1,0:T(8,128)(2,1)S(1)}, bf16[32,3072]{1,0:T(8,128)(2,1)S(1)}, u32[]{:S(2)}, u32[]{:S(2)}) collective-permute-start(bf16[32,3072]{1,0:T(8,128)(2,1)S(1)} %convolution_convert_fusion.4), channel_id=1, source_target_pairs={{6,0},{0,2},{2,4},{4,6},{7,1},{1,3},{3,5},{5,7},{14,8},{8,10},{10,... | collective-permute-start | bytes 589832 | tf_op jit(solution)/shard_map/ppermute | solution.py:22
  13.0 6.1 %collective-permute-start.4 = (bf16[32,3072]{1,0:T(8,128)(2,1)S(1)}, bf16[32,3072]{1,0:T(8,128)(2,1)S(1)}, u32[]{:S(2)}, u32[]{:S(2)}) collective-permute-start(bf16[32,3072]{1,0:T(8,128)(2,1)S(1)} %collective-permute-done.1), channel_id=1, source_target_pairs={{1,0},{0,1},{3,2},{2,3},{5,4},{4,5},{7,6},{6,7},{9,8},{8,9},{11,10... | collective-permute-start | bytes 589832 | tf_op jit(solution)/shard_map/ppermute | solution.py:22
  14.6 51.8 %collective-permute-start.7 = (bf16[64,3072]{1,0:T(8,128)(2,1)S(1)}, bf16[64,3072]{1,0:T(8,128)(2,1)S(1)}, u32[]{:S(2)}, u32[]{:S(2)}) collective-permute-start(bf16[64,3072]{1,0:T(8,128)(2,1)S(1)} %pad_maximum_fusion.refs_0_), channel_id=1, source_target_pairs={{16,0},{24,8},{0,16},{8,24},{17,1},{25,9},{1,17},{9,25},{18,2},{26... | collective-permute-start | bytes 1179656 | tf_op jit(solution)/shard_map/ppermute | solution.py:22
  17.2 49.2 %collective-permute-start.6 = (bf16[64,3072]{1,0:T(8,128)(2,1)S(1)}, bf16[64,3072]{1,0:T(8,128)(2,1)S(1)}, u32[]{:S(2)}, u32[]{:S(2)}) collective-permute-start(bf16[64,3072]{1,0:T(8,128)(2,1)S(1)} %pad_maximum_fusion.refs_0_), channel_id=1, source_target_pairs={{24,0},{0,8},{8,16},{16,24},{25,1},{1,9},{9,17},{17,25},{26,2},{2,... | collective-permute-start | bytes 1179656 | tf_op jit(solution)/shard_map/ppermute | solution.py:22
  17.2 32.2 %collective-permute-start.5 = (bf16[64,3072]{1,0:T(8,128)(2,1)S(1)}, bf16[64,3072]{1,0:T(8,128)(2,1)S(1)}, u32[]{:S(2)}, u32[]{:S(2)}) collective-permute-start(bf16[64,3072]{1,0:T(8,128)(2,1)S(1)} %pad_maximum_fusion.refs_0_), channel_id=1, source_target_pairs={{8,0},{16,8},{24,16},{0,24},{9,1},{17,9},{25,17},{1,25},{10,2},{18... | collective-permute-start | bytes 1179656 | tf_op jit(solution)/shard_map/ppermute | solution.py:22
  19.2 69.6 %collective-permute-start.10 = (bf16[64,3072]{1,0:T(8,128)(2,1)S(1)}, bf16[64,3072]{1,0:T(8,128)(2,1)S(1)}, u32[]{:S(2)}, u32[]{:S(2)}) collective-permute-start(bf16[64,3072]{1,0:T(8,128)(2,1)S(1)} %pad_maximum_fusion.refs_0_), channel_id=1, source_target_pairs={{1,0},{0,1},{3,2},{2,3},{5,4},{4,5},{7,6},{6,7},{9,8},{8,9},{11,10... | collective-permute-start | bytes 1179656 | tf_op jit(solution)/shard_map/ppermute | solution.py:22
  49.4 17.0 %collective-permute-start.8 = (bf16[64,3072]{1,0:T(8,128)(2,1)S(1)}, bf16[64,3072]{1,0:T(8,128)(2,1)S(1)}, u32[]{:S(2)}, u32[]{:S(2)}) collective-permute-start(bf16[64,3072]{1,0:T(8,128)(2,1)S(1)} %collective-permute-done.5.refs_6_), channel_id=1, source_target_pairs={{1,0},{0,1},{3,2},{2,3},{5,4},{4,5},{7,6},{6,7},{9,8},{8,9},{11,10... | collective-permute-start | bytes 1179656 | tf_op jit(solution)/shard_map/ppermute | solution.py:22
  66.4 22.4 %collective-permute-start.11 = (bf16[64,3072]{1,0:T(8,128)(2,1)S(1)}, bf16[64,3072]{1,0:T(8,128)(2,1)S(1)}, u32[]{:S(2)}, u32[]{:S(2)}) collective-permute-start(bf16[64,3072]{1,0:T(8,128)(2,1)S(1)} %collective-permute-done.6.refs_2_), channel_id=1, source_target_pairs={{1,0},{0,1},{3,2},{2,3},{5,4},{4,5},{7,6},{6,7},{9,8},{8,9},{11,10... | collective-permute-start | bytes 1179656 | tf_op jit(solution)/shard_map/ppermute | solution.py:22
  68.0 20.8 %collective-permute-start.12 = (bf16[64,3072]{1,0:T(8,128)(2,1)S(1)}, bf16[64,3072]{1,0:T(8,128)(2,1)S(1)}, u32[]{:S(2)}, u32[]{:S(2)}) collective-permute-start(bf16[64,3072]{1,0:T(8,128)(2,1)S(1)} %collective-permute-done.7.refs_4_), channel_id=1, source_target_pairs={{1,0},{0,1},{3,2},{2,3},{5,4},{4,5},{7,6},{6,7},{9,8},{8,9},{11,10... | collective-permute-start | bytes 1179656 | tf_op jit(solution)/shard_map/ppermute | solution.py:22
  68.5 20.3 %collective-permute-start.9 = (bf16[32,3072]{1,0:T(8,128)(2,1)S(1)}, bf16[32,3072]{1,0:T(8,128)(2,1)S(1)}, u32[]{:S(2)}, u32[]{:S(2)}) collective-permute-start(bf16[32,3072]{1,0:T(8,128)(2,1)S(1)} %slice.13), channel_id=1, source_target_pairs={{1,0},{0,1},{3,2},{2,3},{5,4},{4,5},{7,6},{6,7},{9,8},{8,9},{11,10... | collective-permute-start | bytes 589832 | tf_op jit(solution)/shard_map/ppermute | solution.py:22
  88.9 40.4 %copy-start.3 = (f32[1,128]{1,0:T(1,128)S(1)}, f32[1,128]{1,0:T(1,128)}, u32[]{:S(2)}) copy-start(f32[1,128]{1,0:T(1,128)} %param.12) | copy-start | bytes 1540
  88.9 40.4 %copy-start.4 = (s32[1,128]{1,0:T(1,128)S(1)}, s32[1,128]{1,0:T(1,128)}, u32[]{:S(2)}) copy-start(s32[1,128]{1,0:T(1,128)} %param.11) | copy-start | bytes 1540
  88.9 44.5 %copy-start.2 = (s32[1,128]{1,0:T(1,128)S(1)}, s32[1,128]{1,0:T(1,128)}, u32[]{:S(2)}) copy-start(s32[1,128]{1,0:T(1,128)} %param.14) | copy-start | bytes 1540
  88.9 46.2 %copy-start.1 = (bf16[1,128,3072]{2,1,0:T(8,128)(2,1)S(1)}, bf16[1,128,3072]{2,1,0:T(8,128)(2,1)}, u32[]{:S(2)}) copy-start(bf16[1,128,3072]{2,1,0:T(8,128)(2,1)} %param.13) | copy-start | bytes 2359300
  127.7 5.7 %collective-permute-start.13 = (bf16[32,3072]{1,0:T(8,128)(2,1)S(1)}, bf16[32,3072]{1,0:T(8,128)(2,1)S(1)}, u32[]{:S(2)}, u32[]{:S(2)}) collective-permute-start(bf16[32,3072]{1,0:T(8,128)(2,1)S(1)} %slice.15), channel_id=1, source_target_pairs={{1,0},{0,1},{3,2},{2,3},{5,4},{4,5},{7,6},{6,7},{9,8},{8,9},{11,10... | collective-permute-start | bytes 589832 | tf_op jit(solution)/shard_map/ppermute | solution.py:22
